TPU v7x, 32 devices: a whole 2x2x4 slice. The times are simulated.
32 devices in a mesh: seq: 8 (over z, x), dp: 4 (over y, core).
Axes of the slice: x: 2, y: 2, z: 4, core: 2. Of those that a mesh axis runs over, the one named last changes fastest.
Arguments:
- frames_in: bfloat16 [32, 512, 1024], P('dp', 'seq'), parts along dimension 0, may hold values from -6 to 6
- noise: bfloat16 [32, 512, 1024], P('dp', 'seq'), parts along dimension 0, may hold values from -6 to 6
- lengths: int32 [32], P('dp'), parts along dimension 0, may hold values from 128 to 512, as said below
- span_starts: int32 [32, 16], P('dp'), parts along dimension 0, may hold values from 0 to 502
- w_in1: bfloat16 [1024, 4096], P('seq'), may hold values from -0.1875 to 0.1875
- w_out1: bfloat16 [4096, 1024], P('seq'), may hold values from -0.09375 to 0.09375
- w_qkv: bfloat16 [1024, 3072], P('seq'), may hold values from -0.1875 to 0.1875
- w_attn: bfloat16 [1024, 1024], P('seq'), may hold values from -0.75 to 0.75
- w_point1: bfloat16 [1024, 2048], P('seq'), may hold values from -0.1875 to 0.1875
- w_point2: bfloat16 [1024, 1024], P('seq'), may hold values from -0.5 to 0.5
- w_in2: bfloat16 [1024, 4096], P('seq'), may hold values from -0.1875 to 0.1875
- w_out2: bfloat16 [4096, 1024], P('seq'), may hold values from -0.09375 to 0.09375
- norm_params: float32 [6, 2, 1024], replicated
- kernel: float32 [5, 1024], replicated, may hold values from -2.5 to 2.5
- slopes: float32 [8], replicated, may hold values from 0.3 to 3
- cotangent: bfloat16 [32, 512, 1024], P('dp', 'seq'), parts along dimension 0, may hold values from -6 to 6
Outputs:
- block_out: bfloat16 [32, 512, 1024], P('dp', 'seq'), parts along dimension 0
- grad_frames: float32 [32, 512, 1024], P('dp', 'seq'), parts along dimension 0
- grad_in1: float32 [4096, 4096], P(('dp', 'seq')), parts along dimension 0
- grad_out1: float32 [16384, 1024], P(('dp', 'seq')), parts along dimension 0
- grad_qkv: float32 [4096, 3072], P(('dp', 'seq')), parts along dimension 0
- grad_attn: float32 [4096, 1024], P(('dp', 'seq')), parts along dimension 0
- grad_point1: float32 [4096, 2048], P(('dp', 'seq')), parts along dimension 0
- grad_point2: float32 [4096, 1024], P(('dp', 'seq')), parts along dimension 0
- grad_in2: float32 [4096, 4096], P(('dp', 'seq')), parts along dimension 0
- grad_out2: float32 [16384, 1024], P(('dp', 'seq')), parts along dimension 0
- grad_norms: float32 [24, 2, 1024], P('dp'), parts along dimension 0
- grad_kernel: float32 [20, 1024], P('dp'), parts along dimension 0
- grad_slopes: float32 [32], P('dp'), parts along dimension 0
There are 4 independent parts, one for each index of `dp`. A program takes and returns all parts, laid end to end along the dimension named above; an argument that names none is the same for every part. Nothing has to cross between parts.
Inputs may be any that keep to these rules, and one draw needn't show every extreme that they name: `lengths`: every utterance keeps at least 128 frames, and one utterance of each group keeps all 512. `span_starts`: each span covers 10 frames from its start; spans may intersect.
All inputs are finite; a program needn't handle non-finite values.
Results may differ from a plain program's by a relative error of at most 0.034.
Values may be sent and summed in bfloat16 or wider, within the bound.
A program may use at most 512 MiB of HBM per device.

v0:
```python
import jax
import jax.numpy as jnp
from jax import lax
from jax.sharding import PartitionSpec as P

SPAN = 10


EPSILON = 1e-05
NEGATIVE = -1e30


def padded_2(shard, sides, width):
    for axis, dim in sides:
        peers, length = (lax.axis_size(axis), shard.shape[dim])
        up = [(i, (i + 1) % peers) for i in range(peers - 1)]
        down = [(j, i) for i, j in up]
        last = lax.slice_in_dim(shard, length - width, length, axis=dim)
        initial = lax.slice_in_dim(shard, 0, width, axis=dim)
        before = lax.ppermute(last, axis, up)
        after = lax.ppermute(initial, axis, down)
        shard = jnp.concatenate([before, shard, after], axis=dim)
    return shard


def layer_norm(inputs, gain_vec, shift_vec):
    average = jnp.mean(inputs, axis=-1, keepdims=True)
    centred = inputs - average
    variance = jnp.mean(centred * centred, axis=-1, keepdims=True)
    return centred * lax.rsqrt(variance + EPSILON) * gain_vec + shift_vec


def swish_norm(inputs, gain_vec, shift_vec):
    return jax.nn.silu(layer_norm(inputs, gain_vec, shift_vec))


def glu_gate(joined, live_rows):
    half_width = joined.shape[-1] // 2
    return joined[..., :half_width] * jax.nn.sigmoid(joined[..., half_width:]) * live_rows


def matmul(left_side, right_side):
    return jnp.dot(left_side, right_side, preferred_element_type=jnp.float32)


def matmul_right_t(left_side, right_side):
    return lax.dot_general(
        left_side, right_side, (((1,), (1,)), ((), ())), preferred_element_type=jnp.float32
    )


def matmul_left_t(left_side, right_side):
    return lax.dot_general(
        left_side, right_side, (((0,), (0,)), ((), ())), preferred_element_type=jnp.float32
    )


def block_scores(queries, keys, query_pos, key_pos, key_live, slopes, seq_length):
    factor = queries.shape[-1] ** (-0.5)
    scores = (
        jnp.einsum("uqhd,ukhd->uhqk", queries, keys, preferred_element_type=jnp.float32) * factor
    )
    distance = jnp.abs(query_pos[:, None] - key_pos[None, :]).astype(jnp.float32) / seq_length
    scores = scores - slopes[None, :, None, None] * distance[None, None]
    return (jnp.where(key_live[:, None, None, :], scores, NEGATIVE), distance)


def per_device(
    frames_in,
    noise,
    lengths,
    span_starts,
    w_in1,
    w_out1,
    w_qkv,
    w_attn,
    w_point1,
    w_point2,
    w_in2,
    w_out2,
    norm_params,
    kernel,
    slopes,
    cotangent,
):
    utterances, frames, model_width = frames_in.shape
    head_count = slopes.shape[0]
    head_dim = model_width // head_count
    row_count = utterances * frames
    tap_count = kernel.shape[0]
    half_taps = tap_count // 2
    factor = head_dim ** (-0.5)
    seq_length = frames * lax.axis_size("seq")
    first_frame = lax.axis_index("seq") * frames
    frame_pos = first_frame + jnp.arange(frames, dtype=jnp.int32)
    live_mask = frame_pos[None, :] < lengths[:, None]
    live_rows = live_mask.astype(jnp.float32).reshape(row_count, 1)
    span_begin = span_starts[:, :, None]
    masked = jnp.any(
        (span_begin <= frame_pos[None, None, :]) & (frame_pos[None, None, :] < span_begin + SPAN),
        axis=1,
    )
    start_in = (
        jnp.where(masked[..., None], noise, frames_in)
        .astype(jnp.float32)
        .reshape(row_count, model_width)
    )
    norm_gain = norm_params[:, 0]
    norm_shift = norm_params[:, 1]
    shards = (w_in1, w_out1, w_qkv, w_attn, w_point1, w_point2, w_in2, w_out2)
    gathered = (
        lax.all_gather(shards[0], "seq", axis=0, tiled=True),
        lax.all_gather(shards[1], "seq", axis=0, tiled=True),
        lax.all_gather(shards[2], "seq", axis=0, tiled=True),
        lax.all_gather(shards[3], "seq", axis=0, tiled=True),
        lax.all_gather(shards[4], "seq", axis=0, tiled=True),
        lax.all_gather(shards[5], "seq", axis=0, tiled=True),
        lax.all_gather(shards[6], "seq", axis=0, tiled=True),
        lax.all_gather(shards[7], "seq", axis=0, tiled=True),
    )
    full_in1, full_out1, full_qkv, full_attn, full_point1, full_point2, full_in2, full_out2 = (
        gathered
    )
    act_one = layer_norm(start_in, norm_gain[0], norm_shift[0]).astype(jnp.bfloat16)
    up_one = matmul(act_one, full_in1)
    hid_one = jax.nn.silu(up_one).astype(jnp.bfloat16)
    ffn_one = matmul(hid_one, full_out1)
    resid_one = start_in + 0.5 * ffn_one
    act_two = layer_norm(resid_one, norm_gain[1], norm_shift[1]).astype(jnp.bfloat16)
    packed = (
        matmul(act_two, full_qkv)
        .astype(jnp.bfloat16)
        .reshape(utterances, frames, 3, head_count, head_dim)
    )
    queries = packed[:, :, 0]
    keys = packed[:, :, 1]
    values = packed[:, :, 2]
    row_max = jnp.full((utterances, head_count, frames), NEGATIVE, jnp.float32)
    key_blk = lax.all_gather(keys, "seq", axis=1, tiled=True)
    value_blk = lax.all_gather(values, "seq", axis=1, tiled=True)
    amount = key_blk.shape[1]
    key_pos = jnp.arange(amount, dtype=jnp.int32)
    key_live = key_pos[None, :] < lengths[:, None]
    scores, distance = block_scores(
        queries, key_blk, frame_pos, key_pos, key_live, slopes, seq_length
    )
    new_max = jnp.maximum(row_max, jnp.max(scores, axis=-1))
    expd = jnp.exp(scores - new_max[..., None])
    row_sum = jnp.sum(expd, axis=-1)
    update = jnp.einsum(
        "uhqk,ukhd->uqhd", expd.astype(jnp.bfloat16), value_blk, preferred_element_type=jnp.float32
    )
    partial_value = update
    row_max, row_sum, partial_value = (new_max, row_sum, partial_value)
    attn_out = partial_value / jnp.transpose(row_sum, (0, 2, 1))[..., None]
    log_total = jnp.transpose(row_max + jnp.log(row_sum), (0, 2, 1))
    attn_low = attn_out.astype(jnp.bfloat16).reshape(row_count, model_width)
    attended = matmul(attn_low, full_attn)
    resid_two = resid_one + attended
    act_three = layer_norm(resid_two, norm_gain[2], norm_shift[2]).astype(jnp.bfloat16)
    joined = matmul(act_three, full_point1)
    gated = (
        glu_gate(joined, live_rows).astype(jnp.bfloat16).reshape(utterances, frames, model_width)
    )
    padded = padded_2(gated, (("seq", 1),), half_taps)
    depth = kernel[0] * padded[:, 0:frames].astype(jnp.float32)
    for position in range(1, tap_count):
        depth = depth + kernel[position] * padded[:, position : position + frames].astype(
            jnp.float32
        )
    depth = depth.reshape(row_count, model_width)
    act_four = swish_norm(depth, norm_gain[3], norm_shift[3]).astype(jnp.bfloat16)
    convolved = matmul(act_four, full_point2)
    resid_three = resid_two + convolved
    act_five = layer_norm(resid_three, norm_gain[4], norm_shift[4]).astype(jnp.bfloat16)
    up_two = matmul(act_five, full_in2)
    hid_two = jax.nn.silu(up_two).astype(jnp.bfloat16)
    ffn_two = matmul(hid_two, full_out2)
    resid_four = resid_three + 0.5 * ffn_two
    result = layer_norm(resid_four, norm_gain[5], norm_shift[5])
    gathered = (
        lax.all_gather(shards[0], "seq", axis=0, tiled=True),
        lax.all_gather(shards[1], "seq", axis=0, tiled=True),
        lax.all_gather(shards[2], "seq", axis=0, tiled=True),
        lax.all_gather(shards[3], "seq", axis=0, tiled=True),
        lax.all_gather(shards[4], "seq", axis=0, tiled=True),
        lax.all_gather(shards[5], "seq", axis=0, tiled=True),
        lax.all_gather(shards[6], "seq", axis=0, tiled=True),
        lax.all_gather(shards[7], "seq", axis=0, tiled=True),
    )
    full_in1, full_out1, full_qkv, full_attn, full_point1, full_point2, full_in2, full_out2 = (
        gathered
    )
    grad_result = cotangent.astype(jnp.float32).reshape(row_count, model_width)
    _, back_five = jax.vjp(layer_norm, resid_four, norm_gain[5], norm_shift[5])
    grad_four, gain_five, shift_five = back_five(grad_result)
    grad_ffn2 = (0.5 * grad_four).astype(jnp.bfloat16)
    _, back_silu2 = jax.vjp(jax.nn.silu, up_two)
    grad_up2 = back_silu2(matmul_right_t(grad_ffn2, full_out2))[0].astype(jnp.bfloat16)
    _, back_four = jax.vjp(layer_norm, resid_three, norm_gain[4], norm_shift[4])
    grad_norm4, gain_four, shift_four = back_four(matmul_right_t(grad_up2, full_in2))
    grad_three = grad_four + grad_norm4
    grad_conv = grad_three.astype(jnp.bfloat16)
    _, back_swish = jax.vjp(swish_norm, depth, norm_gain[3], norm_shift[3])
    grad_depth_f, gain_three, shift_three = back_swish(matmul_right_t(grad_conv, full_point2))
    grad_depth = grad_depth_f.astype(jnp.bfloat16).reshape(utterances, frames, model_width)
    grad_padded = padded_2(grad_depth, (("seq", 1),), half_taps)
    grad_depth_wide = grad_depth.astype(jnp.float32)
    grad_gated = jnp.zeros((utterances, frames, model_width), jnp.float32)
    kernel_rows = []
    for position in range(tap_count):
        lower = 2 * half_taps - position
        grad_gated = grad_gated + kernel[position] * grad_padded[:, lower : lower + frames].astype(
            jnp.float32
        )
        kernel_rows.append(
            jnp.sum(
                grad_depth_wide * padded[:, position : position + frames].astype(jnp.float32),
                axis=(0, 1),
            )
        )
    grad_kernel = jnp.stack(kernel_rows)
    _, back_gate = jax.vjp(lambda joined_in: glu_gate(joined_in, live_rows), joined)
    grad_joined = back_gate(grad_gated.reshape(row_count, model_width))[0].astype(jnp.bfloat16)
    _, back_three = jax.vjp(layer_norm, resid_two, norm_gain[2], norm_shift[2])
    grad_norm3, gain_two, shift_two = back_three(matmul_right_t(grad_joined, full_point1))
    grad_two = grad_three + grad_norm3
    grad_att = grad_two.astype(jnp.bfloat16)
    grad_heads = (
        matmul_right_t(grad_att, full_attn)
        .astype(jnp.bfloat16)
        .reshape(utterances, frames, head_count, head_dim)
    )
    spread = jnp.sum(grad_heads.astype(jnp.float32) * attn_out, axis=-1)
    log_total_t = jnp.transpose(log_total, (0, 2, 1))
    spread_t = jnp.transpose(spread, (0, 2, 1))
    grad_slope = jnp.zeros((head_count,), jnp.float32)
    key_blk = lax.all_gather(keys, "seq", axis=1, tiled=True)
    value_blk = lax.all_gather(values, "seq", axis=1, tiled=True)
    amount = key_blk.shape[1]
    key_pos = jnp.arange(amount, dtype=jnp.int32)
    key_live = key_pos[None, :] < lengths[:, None]
    scores, distance = block_scores(
        queries, key_blk, frame_pos, key_pos, key_live, slopes, seq_length
    )
    attn_prob = jnp.exp(scores - log_total_t[..., None])
    grad_prob = jnp.einsum(
        "uqhd,ukhd->uhqk", grad_heads, value_blk, preferred_element_type=jnp.float32
    )
    grad_exact = attn_prob * (grad_prob - spread_t[..., None])
    grad_scores = grad_exact.astype(jnp.bfloat16)
    grad_query = (
        jnp.einsum("uhqk,ukhd->uqhd", grad_scores, key_blk, preferred_element_type=jnp.float32)
        * factor
    )
    grad_slope = grad_slope - jnp.sum(grad_exact * distance[None, None], axis=(0, 2, 3))
    grad_query, grad_slope = (grad_query, grad_slope)
    query_blk = lax.all_gather(queries, "seq", axis=1, tiled=True)
    dhead_blk = lax.all_gather(grad_heads, "seq", axis=1, tiled=True)
    total_blk = lax.all_gather(log_total.astype(jnp.bfloat16), "seq", axis=1, tiled=True).astype(
        jnp.float32
    )
    spread_blk = lax.all_gather(spread.astype(jnp.bfloat16), "seq", axis=1, tiled=True).astype(
        jnp.float32
    )
    amount = query_blk.shape[1]
    query_pos = jnp.arange(amount, dtype=jnp.int32)
    scores, distance = block_scores(
        query_blk, keys, query_pos, frame_pos, live_mask, slopes, seq_length
    )
    attn_prob = jnp.exp(scores - jnp.transpose(total_blk, (0, 2, 1))[..., None])
    grad_value = jnp.einsum(
        "uhqk,uqhd->ukhd",
        attn_prob.astype(jnp.bfloat16),
        dhead_blk,
        preferred_element_type=jnp.float32,
    )
    grad_prob = jnp.einsum("uqhd,ukhd->uhqk", dhead_blk, values, preferred_element_type=jnp.float32)
    grad_scores = (
        attn_prob * (grad_prob - jnp.transpose(spread_blk, (0, 2, 1))[..., None])
    ).astype(jnp.bfloat16)
    grad_key = (
        jnp.einsum("uhqk,uqhd->ukhd", grad_scores, query_blk, preferred_element_type=jnp.float32)
        * factor
    )
    grad_key, grad_value = (grad_key, grad_value)
    grad_packed = (
        jnp.stack([grad_query, grad_key, grad_value], axis=2)
        .astype(jnp.bfloat16)
        .reshape(row_count, 3 * model_width)
    )
    _, back_two = jax.vjp(layer_norm, resid_one, norm_gain[1], norm_shift[1])
    grad_norm2, gain_one, shift_one = back_two(matmul_right_t(grad_packed, full_qkv))
    grad_one = grad_two + grad_norm2
    grad_ffn1 = (0.5 * grad_one).astype(jnp.bfloat16)
    _, back_silu1 = jax.vjp(jax.nn.silu, up_one)
    grad_up1 = back_silu1(matmul_right_t(grad_ffn1, full_out1))[0].astype(jnp.bfloat16)
    _, back_one = jax.vjp(layer_norm, start_in, norm_gain[0], norm_shift[0])
    grad_norm1, gain_zero, shift_zero = back_one(matmul_right_t(grad_up1, full_in1))
    grad_start = grad_one + grad_norm1
    grad_frames = jnp.where(
        masked[..., None], 0.0, grad_start.reshape(utterances, frames, model_width)
    )
    wide_pairs = (
        (act_one, grad_up1),
        (act_two, grad_packed),
        (attn_low, grad_att),
        (act_three, grad_joined),
        (act_four, grad_conv),
        (act_five, grad_up2),
    )
    wide = lax.psum_scatter(
        jnp.concatenate(
            [matmul_left_t(left_side, right_side) for left_side, right_side in wide_pairs], axis=1
        ).astype(jnp.bfloat16),
        "seq",
        scatter_dimension=0,
        tiled=True,
    ).astype(jnp.float32)
    tall_pairs = ((hid_one, grad_ffn1), (hid_two, grad_ffn2))
    tall = lax.psum_scatter(
        jnp.concatenate(
            [matmul_left_t(left_side, right_side) for left_side, right_side in tall_pairs], axis=1
        ).astype(jnp.bfloat16),
        "seq",
        scatter_dimension=0,
        tiled=True,
    ).astype(jnp.float32)
    hidden_width = w_in1.shape[1]
    column_cuts = [
        hidden_width,
        3 * model_width,
        model_width,
        2 * model_width,
        model_width,
        hidden_width,
    ]
    wide_parts = []
    column_start = 0
    for column_width in column_cuts:
        wide_parts.append(wide[:, column_start : column_start + column_width])
        column_start = column_start + column_width
    grad_in1, grad_qkv, grad_attn, grad_point1, grad_point2, grad_in2 = wide_parts
    grad_out1 = tall[:, :model_width]
    grad_out2 = tall[:, model_width:]
    grad_norms = jnp.stack(
        [
            jnp.stack([gain_zero, shift_zero]),
            jnp.stack([gain_one, shift_one]),
            jnp.stack([gain_two, shift_two]),
            jnp.stack([gain_three, shift_three]),
            jnp.stack([gain_four, shift_four]),
            jnp.stack([gain_five, shift_five]),
        ]
    )
    grad_norms, grad_kernel, grad_slope = (
        lax.psum(grad_norms.astype(jnp.bfloat16), "seq").astype(jnp.float32),
        lax.psum(grad_kernel.astype(jnp.bfloat16), "seq").astype(jnp.float32),
        lax.psum(grad_slope.astype(jnp.bfloat16), "seq").astype(jnp.float32),
    )
    block_out = result.astype(jnp.bfloat16).reshape(utterances, frames, model_width)
    return (
        block_out,
        grad_frames,
        grad_in1,
        grad_out1,
        grad_qkv,
        grad_attn,
        grad_point1,
        grad_point2,
        grad_in2,
        grad_out2,
        grad_norms,
        grad_kernel,
        grad_slope,
    )


def solution(mesh):
    in_specs = (
        P("dp", "seq", None),
        P("dp", "seq", None),
        P("dp"),
        P("dp", None),
        P("seq", None),
        P("seq", None),
        P("seq", None),
        P("seq", None),
        P("seq", None),
        P("seq", None),
        P("seq", None),
        P("seq", None),
        P(),
        P(),
        P(),
        P("dp", "seq", None),
    )
    out_specs = (
        P("dp", "seq", None),
        P("dp", "seq", None),
        P(("dp", "seq"), None),
        P(("dp", "seq"), None),
        P(("dp", "seq"), None),
        P(("dp", "seq"), None),
        P(("dp", "seq"), None),
        P(("dp", "seq"), None),
        P(("dp", "seq"), None),
        P(("dp", "seq"), None),
        P("dp", None, None),
        P("dp", None),
        P("dp"),
    )
    return jax.shard_map(
        per_device, mesh=mesh, in_specs=in_specs, out_specs=out_specs, check_vma=False
    )
```

profile of v0, /device:TPU:1, one launch (start us, length us, event | category | flops | bytes accessed | tf_op | source)
XLA Modules:
  0.0 2182.7 jit_solution(2001288699346939952)
XLA Ops:
  11.9 124.9 %all-gather.16.cloned.1.call-done = bf16[1024,4096]{1,0:T(8,128)(2,1)} async-done(((bf16[128,4096]{1,0:T(8,128)(2,1)}), bf16[1024,4096]{1,0:T(8,128)(2,1)}) %all-gather.16.cloned.1.call-update) | async-done | bytes 8388624 | tf_op jit(solution)/shard_map/all_gather | solution.py:112
  146.8 115.3 %all-gather.18.cloned.1.call-done = bf16[4096,1024]{1,0:T(8,128)(2,1)} async-done(((bf16[512,1024]{1,0:T(8,128)(2,1)}), bf16[4096,1024]{1,0:T(8,128)(2,1)}) %all-gather.18.cloned.1.call-update) | async-done | bytes 8388624 | tf_op jit(solution)/shard_map/all_gather | solution.py:113
  272.2 89.2 %all-gather.20.cloned.1.call-done = bf16[1024,3072]{1,0:T(8,128)(2,1)} async-done(((bf16[128,3072]{1,0:T(8,128)(2,1)}), bf16[1024,3072]{1,0:T(8,128)(2,1)}) %all-gather.20.cloned.1.call-update) | async-done | bytes 6291472 | tf_op jit(solution)/shard_map/all_gather | solution.py:114
  381.7 114.4 %all-gather.36.cloned.1.call-done = bf16[8,512,1,8,128]{4,1,3,0,2:T(8,128)(2,1)} async-done(((bf16[8,64,1,8,128]{4,1,3,0,2:T(8,128)(2,1)}), bf16[8,512,1,8,128]{4,1,3,0,2:T(8,128)(2,1)}) %all-gather.36.cloned.1.call-update) | async-done | bytes 8388624 | tf_op jit(solution)/shard_map/all_gather | solution.py:139
  508.3 113.6 %all-gather.34.cloned.1.call-done = bf16[8,512,1,8,128]{4,1,3,0,2:T(8,128)(2,1)} async-done(((bf16[8,64,1,8,128]{4,1,3,0,2:T(8,128)(2,1)}), bf16[8,512,1,8,128]{4,1,3,0,2:T(8,128)(2,1)}) %all-gather.34.cloned.1.call-update) | async-done | bytes 8388624 | tf_op jit(solution)/shard_map/all_gather | solution.py:140
  632.6 38.1 %all-gather.22.cloned.1.call-done = bf16[1024,1024]{1,0:T(8,128)(2,1)} async-done(((bf16[128,1024]{1,0:T(8,128)(2,1)}), bf16[1024,1024]{1,0:T(8,128)(2,1)}) %all-gather.22.cloned.1.call-update) | async-done | bytes 2097168 | tf_op jit(solution)/shard_map/all_gather | solution.py:115
  675.7 69.0 %all-gather.24.cloned.1.call-done = bf16[1024,2048]{1,0:T(8,128)(2,1)} async-done(((bf16[128,2048]{1,0:T(8,128)(2,1)}), bf16[1024,2048]{1,0:T(8,128)(2,1)}) %all-gather.24.cloned.1.call-update) | async-done | bytes 4194320 | tf_op jit(solution)/shard_map/all_gather | solution.py:116
  763.9 31.6 %all-gather.26.cloned.1.call-done = bf16[1024,1024]{1,0:T(8,128)(2,1)} async-done(((bf16[128,1024]{1,0:T(8,128)(2,1)}), bf16[1024,1024]{1,0:T(8,128)(2,1)}) %all-gather.26.cloned.1.call-update) | async-done | bytes 2097168 | tf_op jit(solution)/shard_map/all_gather | solution.py:117
  800.7 121.0 %all-gather.28.cloned.1.call-done = bf16[1024,4096]{1,0:T(8,128)(2,1)} async-done(((bf16[128,4096]{1,0:T(8,128)(2,1)}), bf16[1024,4096]{1,0:T(8,128)(2,1)}) %all-gather.28.cloned.1.call-update) | async-done | bytes 8388624 | tf_op jit(solution)/shard_map/all_gather | solution.py:118
  921.8 12.1 fusion.145
  933.8 113.1 %all-gather.30.cloned.1.call-done = bf16[4096,1024]{1,0:T(8,128)(2,1)} async-done(((bf16[512,1024]{1,0:T(8,128)(2,1)}), bf16[4096,1024]{1,0:T(8,128)(2,1)}) %all-gather.30.cloned.1.call-update) | async-done | bytes 8388624 | tf_op jit(solution)/shard_map/all_gather | solution.py:119
  1046.9 11.0 fusion.166
  1062.5 13.7 fusion.2
  1115.6 34.9 %all_gather.63 = bf16[8,512,8]{2,0,1:T(8,128)(2,1)S(1)} all-gather(bf16[8,64,8]{2,0,1:T(8,128)(2,1)S(1)} %copy.88), channel_id=1, replica_groups=mesh['seq'=8,'dp'=4] {'seq'}, dimensions={1}, use_global_device_ids=true | all-gather | bytes 73728 | tf_op jit(solution)/shard_map/all_gather | solution.py:260
  1154.1 38.1 %all-gather.38.cloned.1.call-done = bf16[8,512,1,8,128]{4,1,3,0,2:T(8,128)(2,1)} async-done(((bf16[8,64,1,8,128]{4,1,3,0,2:T(8,128)(2,1)}), bf16[8,512,1,8,128]{4,1,3,0,2:T(8,128)(2,1)}) %all-gather.38.cloned.1.call-update) | async-done | bytes 8388624 | tf_op jit(solution)/shard_map/all_gather | solution.py:258
  1202.4 11.2 convolution_convert_fusion
  1214.3 32.2 %all_gather.65 = bf16[8,512,8]{2,0,1:T(8,128)(2,1)S(1)} all-gather(bf16[8,64,8]{2,0,1:T(8,128)(2,1)S(1)} %copy.91), channel_id=1, replica_groups=mesh['seq'=8,'dp'=4] {'seq'}, dimensions={1}, use_global_device_ids=true | all-gather | bytes 73728 | tf_op jit(solution)/shard_map/all_gather | solution.py:263
  1248.0 11.2 multiply_reduce_fusion
  1264.4 62.8 %all-gather.32.cloned.1.call-done = bf16[8,512,8,128]{3,1,2,0:T(8,128)(2,1)} async-done(((bf16[8,64,8,128]{3,1,2,0:T(8,128)(2,1)}), bf16[8,512,8,128]{3,1,2,0:T(8,128)(2,1)}) %all-gather.32.cloned.1.call-update) | async-done | bytes 8388624 | tf_op jit(solution)/shard_map/all_gather | solution.py:259
  1336.3 12.0 fusion.99
  1365.6 11.6 convolution_convert_fusion.1
  1446.0 30.6 %all-reduce.2 = (bf16[6,2,1024]{2,1,0:T(2,128)(2,1)S(1)}, bf16[5,1024]{1,0:T(8,128)(2,1)S(1)}, bf16[8]{0:T(256)(128)(2,1)S(1)}) all-reduce(bf16[6,2,1024]{2,1,0:T(2,128)(2,1)S(1)} %constant_dynamic-update-slice_fusion, bf16[5,1024]{1,0:T(8,128)(2,1)S(1)} %stack.138, ...), channel_id=1, replica_groups=mesh['seq'=8,'dp'=4] {'seq'}, use_global_device_ids=true, to_apply=%region_42.43 | all-reduce | flops 17416 | bytes 69664 | tf_op jit(solution)/shard_map/psum | solution.py:357
  1482.3 188.3 %reduce-scatter.5.cloned.1.call-done = bf16[512,2048]{0,1:T(8,128)(2,1)} async-done(((bf16[4096,2048]{0,1:T(8,128)(2,1)}), bf16[512,2048]{0,1:T(8,128)(2,1)}) %reduce-scatter.5.cloned.1.call-update) | async-done | bytes 2097168 | tf_op jit(solution)/shard_map/reduce_scatter | solution.py:321
  1678.7 489.4 %reduce-scatter.3.cloned.1.call-done = bf16[128,15360]{1,0:T(8,128)(2,1)} async-done(((bf16[1024,15360]{1,0:T(8,128)(2,1)}), bf16[128,15360]{1,0:T(8,128)(2,1)}) %reduce-scatter.3.cloned.1.call-update) | async-done | bytes 3932176 | tf_op jit(solution)/shard_map/reduce_scatter | solution.py:312
  (405 shorter events, 277.6 us)
Async XLA Ops:
  7.2 129.6 %all-gather.16.cloned.1.call-start = ((), (), s32[]{:S(2)}) async-start(), calls=%async_computation.2 | async-start | bytes 9437184 | tf_op jit(solution)/shard_map/all_gather | solution.py:112
  7.9 254.1 %all-gather.18.cloned.1.call-start = ((), (), s32[]{:S(2)}) async-start(), calls=%async_computation.3 | async-start | bytes 9437184 | tf_op jit(solution)/shard_map/all_gather | solution.py:113
  8.7 352.7 %all-gather.20.cloned.1.call-start = ((), (), s32[]{:S(2)}) async-start(), calls=%async_computation.4 | async-start | bytes 7077888 | tf_op jit(solution)/shard_map/all_gather | solution.py:114
  9.4 486.7 %all-gather.36.cloned.1.call-start = ((), (), s32[]{:S(2)}) async-start(), calls=%async_computation.14 | async-start | bytes 9437184 | tf_op jit(solution)/shard_map/all_gather | solution.py:139
  10.9 350.5 %copy-start.71 = (f32[1,1,1024]{2,1,0:T(1,128)}, f32[1,1,1024]{2,1,0:T(1,128)S(1)}, u32[]{:S(2)}) copy-start(f32[1,1,1024]{2,1,0:T(1,128)S(1)} %get-tuple-element.144) | copy-start | bytes 12292
  10.9 350.5 %copy-start.86 = (f32[1,1,1024]{2,1,0:T(1,128)}, f32[1,1,1024]{2,1,0:T(1,128)S(1)}, u32[]{:S(2)}) copy-start(f32[1,1,1024]{2,1,0:T(1,128)S(1)} %get-tuple-element.143) | copy-start | bytes 12292
  10.9 733.8 %copy-start.84 = (f32[1,1,1024]{2,1,0:T(1,128)}, f32[1,1,1024]{2,1,0:T(1,128)S(1)}, u32[]{:S(2)}) copy-start(f32[1,1,1024]{2,1,0:T(1,128)S(1)} %get-tuple-element.141) | copy-start | bytes 12292
  10.9 910.9 %copy-start.82 = (f32[1,1,1024]{2,1,0:T(1,128)}, f32[1,1,1024]{2,1,0:T(1,128)S(1)}, u32[]{:S(2)}) copy-start(f32[1,1,1024]{2,1,0:T(1,128)S(1)} %get-tuple-element.137) | copy-start | bytes 12292
  10.9 1073.4 %copy-start.69 = (f32[1,1,1024]{2,1,0:T(1,128)}, f32[1,1,1024]{2,1,0:T(1,128)S(1)}, u32[]{:S(2)}) copy-start(f32[1,1,1024]{2,1,0:T(1,128)S(1)} %get-tuple-element.138) | copy-start | bytes 12292
  271.8 398.9 %copy-start.14 = (f32[512,1024]{1,0:T(8,128)}, f32[512,1024]{1,0:T(8,128)S(1)}, u32[]{:S(2)}) copy-start(f32[512,1024]{1,0:T(8,128)S(1)} %get-tuple-element.156) | copy-start | bytes 6291460
  372.8 249.2 %all-gather.34.cloned.1.call-start = ((), (), s32[]{:S(2)}) async-start(), calls=%async_computation.13 | async-start | bytes 9437184 | tf_op jit(solution)/shard_map/all_gather | solution.py:140
  375.3 295.4 %all-gather.22.cloned.1.call-start = ((), (), s32[]{:S(2)}) async-start(), calls=%async_computation.5 | async-start | bytes 2359296 | tf_op jit(solution)/shard_map/all_gather | solution.py:115
  375.9 368.8 %all-gather.24.cloned.1.call-start = ((), (), s32[]{:S(2)}) async-start(), calls=%async_computation.6 | async-start | bytes 4718592 | tf_op jit(solution)/shard_map/all_gather | solution.py:116
  376.7 418.8 %all-gather.26.cloned.1.call-start = ((), (), s32[]{:S(2)}) async-start(), calls=%async_computation.7 | async-start | bytes 2359296 | tf_op jit(solution)/shard_map/all_gather | solution.py:117
  377.4 544.3 %all-gather.28.cloned.1.call-start = ((), (), s32[]{:S(2)}) async-start(), calls=%async_computation.8 | async-start | bytes 9437184 | tf_op jit(solution)/shard_map/all_gather | solution.py:118
  378.2 668.7 %all-gather.30.cloned.1.call-start = ((), (), s32[]{:S(2)}) async-start(), calls=%async_computation.9 | async-start | bytes 9437184 | tf_op jit(solution)/shard_map/all_gather | solution.py:119
  378.7 813.5 %all-gather.38.cloned.1.call-start = ((), (), s32[]{:S(2)}) async-start(), calls=%async_computation.15 | async-start | bytes 9437184 | tf_op jit(solution)/shard_map/all_gather | solution.py:258
  752.1 4.8 collective-permute-start
  754.3 5.9 collective-permute-start.1
  756.9 570.3 %all-gather.32.cloned.1.call-start = ((), (), s32[]{:S(2)}) async-start(), calls=%async_computation.10 | async-start | bytes 9437184 | tf_op jit(solution)/shard_map/all_gather | solution.py:259
  1093.1 5.3 collective-permute-start.2
  1094.4 5.0 collective-permute-start.3
  1114.1 556.4 %reduce-scatter.5.cloned.1.call-start = ((), (), s32[]{:S(2)}) async-start(), calls=%async_computation.12 | async-start | bytes 18874368 | tf_op jit(solution)/shard_map/reduce_scatter | solution.py:321
  1387.9 780.2 %reduce-scatter.3.cloned.1.call-start = ((), (), s32[]{:S(2)}) async-start(), calls=%async_computation.11 | async-start | bytes 35389440 | tf_op jit(solution)/shard_map/reduce_scatter | solution.py:312
  (100 other events, 2337.4 us)
Sparse Core Ops, SparseCore 0:
  10.2 126.5 all-gather.15
  138.9 123.1 all-gather.17
  264.3 97.0 all-gather.19
  372.9 123.1 all-gather.35
  498.8 123.1 all-gather.33
  623.9 46.7 all-gather.21
  672.8 71.7 all-gather.23
  746.8 48.6 all-gather.25
  797.6 124.1 all-gather.27
  923.7 123.1 all-gather.29
  1049.1 143.1 all-gather.37
  1194.3 132.8 all-gather.31
  1388.0 282.5 reduce-scatter.4
  1674.8 493.2 reduce-scatter.2
where the time goes:
time: 2190 us; the launch traced here: 2180 us
  waiting for transfers between devices  1720 us (79%)
  matrix products  234 us (11%)
  blocking collectives  97.6 us (4%)
  local copies, waits for them, and re-layouts  58.9 us (3%)
  other arithmetic  48 us (2%)
    reduce_scatter x2, waiting for transfers between devices, per_device(): lax.psum_scatter(jnp.concatenate([matmul_left_t(left_side, right_side) fo...  678 us
    all_gather x1, waiting for transfers between devices, per_device(): lax.all_gather(shards[0], 'seq', axis=0, tiled=True)  125 us
    all_gather x1, waiting for transfers between devices, per_device(): lax.all_gather(shards[6], 'seq', axis=0, tiled=True)  121 us
    all_gather x1, waiting for transfers between devices, per_device(): lax.all_gather(shards[1], 'seq', axis=0, tiled=True)  115 us
    all_gather x1, waiting for transfers between devices, per_device(): key_blk = lax.all_gather(keys, 'seq', axis=1, tiled=True)  114 us
    all_gather x1, waiting for transfers between devices, per_device(): value_blk = lax.all_gather(values, 'seq', axis=1, tiled=True)  114 us
    all_gather x1, waiting for transfers between devices, per_device(): lax.all_gather(shards[7], 'seq', axis=0, tiled=True)  113 us
    all_gather x1, waiting for transfers between devices, per_device(): lax.all_gather(shards[2], 'seq', axis=0, tiled=True)  89.2 us
  transfers between devices with their start and end apart: 18, of which 16 were waited for; matrix products, arithmetic and copies ran while one was open for 11% of the time, Pallas kernels for 0%

commit v1 on v0

--- a/solution.py
+++ b/solution.py
@@ -1,7 +1,16 @@
+import functools
+
 import jax
 import jax.numpy as jnp
 from jax import lax
+from jax.experimental import pallas as pl
+from jax.experimental.pallas import tpu as pltpu
 from jax.sharding import PartitionSpec as P
+
+MESH = pl.DeviceIdType.MESH
+BF16 = jnp.bfloat16
+F32 = jnp.float32
+ANY = pl.BlockSpec(memory_space=pl.ANY)
 
 SPAN = 10
 
@@ -65,7 +74,7 @@
     return (jnp.where(key_live[:, None, None, :], scores, NEGATIVE), distance)
 
 
-def per_device(
+def per_device_any(
     frames_in,
     noise,
     lengths,
@@ -376,6 +385,581 @@
     )
 
 
+def place():
+    seq, dp = lax.axis_index("seq"), lax.axis_index("dp")
+    return seq // 2, lax.rem(seq, 2), dp // 2, lax.rem(dp, 2)
+
+
+def device(z, x, y, core):
+    return (z * 2 + x, y * 2 + core)
+
+
+def z_partners(z):
+    return (z + 1 - 2 * lax.rem(z, 2), lax.rem(z + 2, 4), 3 - z)
+
+
+def remote(source, target, send, recv, where):
+    return pltpu.make_async_remote_copy(
+        src_ref=source,
+        dst_ref=target,
+        send_sem=send,
+        recv_sem=recv,
+        device_id=where,
+        device_id_type=MESH,
+    )
+
+
+def greet(partners, waits):
+    barrier = pltpu.get_barrier_semaphore()
+    for partner in partners:
+        pl.semaphore_signal(barrier, inc=1, device_id=partner, device_id_type=MESH)
+    pl.semaphore_wait(barrier, waits)
+
+
+def utterance_of(z, x, core):
+    return lax.rem(z, 2) * 4 + x * 2 + core
+
+
+def home_of(utterance, y, group):
+    return device(2 * group + utterance // 4, lax.rem(utterance // 2, 2), y, lax.rem(utterance, 2))
+
+
+def bits_of(s):
+    return s // 4, lax.rem(s // 2, 2), lax.rem(s, 2)
+
+
+def flipped(bits, r):
+    flips = (r // 4, r // 2 % 2, r % 2)
+    return [1 - b if f else b for b, f in zip(bits, flips)]
+
+
+def utterance_in_round(seq, r):
+    b2, b1, b0 = bits_of(seq)
+    out = flipped((b1, b0, b2), r)
+    return out[0] * 4 + out[1] * 2 + out[2]
+
+
+def seq_in_round(utterance, r):
+    t2, t1, t0 = flipped(bits_of(utterance), r)
+    return t0 * 4 + t2 * 2 + t1
+
+
+def exchange_kernel(count, to_utterances, *refs):
+    ins, outs = refs[:count], refs[count : 2 * count]
+    send, recv, own = refs[2 * count :]
+    z, x, y, core = place()
+    seq = z * 2 + x
+    group = z // 2
+    utterance = utterance_of(z, x, core)
+    same = group == core
+    seqs = [seq_in_round(utterance, r) for r in range(8)]
+    mates = [utterance_in_round(seq, r) for r in range(8)]
+    sources = [device(s // 2, lax.rem(s, 2), y, group) for s in seqs]
+    homes = [home_of(u, y, core) for u in mates]
+    if to_utterances:
+        targets, givers, mine, blocks = homes, sources, seq, mates
+    else:
+        targets, givers, mine, blocks = sources, homes, utterance, seqs
+    barrier = pltpu.get_barrier_semaphore()
+    for r in range(8):
+        if r == 0:
+
+            @pl.when(jnp.logical_not(same))
+            def _():
+                pl.semaphore_signal(barrier, inc=1, device_id=givers[0], device_id_type=MESH)
+        else:
+            pl.semaphore_signal(barrier, inc=1, device_id=givers[r], device_id_type=MESH)
+    pl.semaphore_wait(barrier, jnp.where(same, 7, 8))
+
+    def copy(i, r):
+        return remote(
+            ins[i].at[blocks[r]], outs[i].at[mine], send.at[i, r], recv.at[i, r], targets[r]
+        )
+
+    def local(i):
+        return pltpu.make_async_copy(ins[i].at[blocks[0]], outs[i].at[mine], own.at[i])
+
+    for i in range(count):
+
+        @pl.when(jnp.logical_not(same))
+        def _():
+            copy(i, 0).start()
+
+        @pl.when(same)
+        def _():
+            local(i).start()
+
+        for r in range(1, 8):
+            copy(i, r).start()
+    for i in range(count):
+
+        @pl.when(jnp.logical_not(same))
+        def _():
+            copy(i, 0).wait()
+
+        @pl.when(same)
+        def _():
+            local(i).wait()
+
+        for r in range(1, 8):
+            copy(i, r).wait()
+
+
+def exchange(arrays, to_utterances, collective_id):
+    count = len(arrays)
+    return pl.pallas_call(
+        functools.partial(exchange_kernel, count, to_utterances),
+        out_shape=[jax.ShapeDtypeStruct(a.shape, a.dtype) for a in arrays],
+        in_specs=[ANY] * count,
+        out_specs=[ANY] * count,
+        scratch_shapes=[
+            pltpu.SemaphoreType.DMA((count, 8)),
+            pltpu.SemaphoreType.DMA((count, 8)),
+            pltpu.SemaphoreType.DMA((count,)),
+        ],
+        compiler_params=pltpu.CompilerParams(collective_id=collective_id, has_side_effects=True),
+    )(*arrays)
+
+
+def units_of(shapes):
+    units = []
+    for index, (rows, columns) in enumerate(shapes):
+        for row in range(0, rows, 128):
+            for column in range(0, columns, 1024):
+                units.append((index, row, column))
+    return units
+
+
+ROWS = 128
+HALF = 64
+COLUMNS = 1024
+SPLIT = 384
+
+
+def gather_kernel(units, count, *refs):
+    shards, fulls = refs[:count], refs[count : 2 * count]
+    send, recv, own = refs[2 * count :]
+    z, x, y, core = place()
+    zs = z_partners(z)
+    over_z = [device(other, x, y, core) for other in zs]
+    over_x = device(z, 1 - x, y, core)
+    over_y = device(z, x, 1 - y, core)
+    over_core = device(z, x, y, 1 - core)
+    greet(over_z + [over_x, over_y, over_core], 6)
+
+    def spot(unit):
+        index, row, column = unit
+        rows = pl.ds(row + pl.multiple_of(core * HALF, HALF), HALF)
+        mine = pl.ds(column + pl.multiple_of(y * SPLIT, 128), COLUMNS - SPLIT)
+        third = pl.ds(column + pl.multiple_of(y * (COLUMNS - SPLIT), 128), SPLIT)
+        return shards[index], fulls[index], rows, mine, third, pl.ds(column, COLUMNS)
+
+    def first(u):
+        shard, full, rows, mine, _, _ = spot(units[u])
+        source = shard.at[rows, mine]
+        out = [pltpu.make_async_copy(source, full.at[z, x, rows, mine], own.at[u])]
+        for j in range(3):
+            out.append(
+                remote(source, full.at[z, x, rows, mine], send.at[u, j], recv.at[u, j], over_z[j])
+            )
+        return out
+
+    def second(u):
+        _, full, rows, mine, _, _ = spot(units[u])
+        piece = full.at[:, x, rows, mine]
+        return [remote(piece, piece, send.at[u, 3], recv.at[u, 3], over_x)]
+
+    def third(u):
+        _, full, rows, _, part, _ = spot(units[u])
+        piece = full.at[:, :, rows, part]
+        return [remote(piece, piece, send.at[u, 4], recv.at[u, 4], over_y)]
+
+    def fourth(u):
+        _, full, rows, _, _, whole = spot(units[u])
+        piece = full.at[:, :, rows, whole]
+        return [remote(piece, piece, send.at[u, 5], recv.at[u, 5], over_core)]
+
+    stages = (first, second, third, fourth)
+    last = len(units)
+    for step in range(last + len(stages)):
+        for depth, stage in enumerate(stages):
+            u = step - depth
+            if depth > 0 and 0 <= u < last:
+                for copy in stages[depth - 1](u):
+                    copy.wait()
+            if 0 <= u < last:
+                for copy in stage(u):
+                    copy.start()
+        u = step - len(stages)
+        if 0 <= u < last:
+            for copy in stages[-1](u):
+                copy.wait()
+
+
+def gather(shards, collective_id):
+    count = len(shards)
+    shapes = [s.shape for s in shards]
+    units = units_of(shapes)
+    fulls = pl.pallas_call(
+        functools.partial(gather_kernel, units, count),
+        out_shape=[jax.ShapeDtypeStruct((4, 2) + s, BF16) for s in shapes],
+        in_specs=[ANY] * count,
+        out_specs=[ANY] * count,
+        scratch_shapes=[
+            pltpu.SemaphoreType.DMA((len(units), 6)),
+            pltpu.SemaphoreType.DMA((len(units), 6)),
+            pltpu.SemaphoreType.DMA((len(units),)),
+        ],
+        compiler_params=pltpu.CompilerParams(collective_id=collective_id, has_side_effects=True),
+    )(*shards)
+    return [f.reshape(8 * s[0], s[1]) for f, s in zip(fulls, shapes)]
+
+
+def scatter_kernel(units, count, *refs):
+    grads, outs = refs[:count], refs[count : 2 * count]
+    (mine, core_in, x_in, z_in, load, s_core, r_core, s_x, r_x, s_z, r_z, s_far, r_far, s_near, r_near, local) = refs[
+        2 * count :
+    ]
+    z, x, y, core = place()
+    group = z // 2
+    z_other = z + 1 - 2 * lax.rem(z, 2)
+    over_core = device(z, x, y, 1 - core)
+    over_x = device(z, 1 - x, y, core)
+    over_z = device(z_other, x, y, core)
+    far = device(3 - z, x, y, group)
+    keeps = core == group
+    barrier = pltpu.get_barrier_semaphore()
+    for partner in (over_core, over_x, over_z):
+        pl.semaphore_signal(barrier, inc=1, device_id=partner, device_id_type=MESH)
+    far_givers = [device(3 - z, x, y, 0), device(3 - z, x, y, 1)]
+
+    @pl.when(jnp.logical_not(keeps))
+    def _():
+        for giver in far_givers:
+            pl.semaphore_signal(barrier, inc=1, device_id=giver, device_id_type=MESH)
+
+    pl.semaphore_wait(barrier, 4)
+
+    half = pl.multiple_of(core * HALF, HALF)
+    other_half = pl.multiple_of((1 - core) * HALF, HALF)
+
+    def core_copy(u):
+        index, row, column = units[u]
+        source = grads[index].at[:, :, pl.ds(row + other_half, HALF), pl.ds(column, COLUMNS)]
+        return remote(source, core_in.at[u % 2], s_core.at[u % 2], r_core.at[u % 2], over_core)
+
+    def load_copy(u):
+        index, row, column = units[u]
+        source = grads[index].at[:, :, pl.ds(row + half, HALF), pl.ds(column, COLUMNS)]
+        return pltpu.make_async_copy(source, mine.at[u % 5], load.at[u % 2])
+
+    def x_copy(u):
+        return remote(
+            mine.at[u % 5, :, 1 - x], x_in.at[u % 4], s_x.at[u % 4], r_x.at[u % 4], over_x
+        )
+
+    def z_copy(u, part):
+        target_z = z_other if part == 0 else 3 - z_other
+        return remote(
+            mine.at[u % 5, target_z, x],
+            z_in.at[u % 4, part],
+            s_z.at[u % 4, part],
+            r_z.at[u % 4, part],
+            over_z,
+        )
+
+    def far_copy(u):
+        index, row, column = units[u]
+        target = outs[index].at[pl.ds(row + half, HALF), pl.ds(column, COLUMNS)]
+        return remote(
+            mine.at[u % 5, 3 - z, x], target, s_far.at[u % 2], r_far.at[u, core], far
+        )
+
+    def far_arrival(u, giver):
+        index, row, column = units[u]
+        target = outs[index].at[pl.ds(row + giver * HALF, HALF), pl.ds(column, COLUMNS)]
+        return remote(
+            mine.at[u % 5, 3 - z, x], target, s_far.at[u % 2], r_far.at[u, giver], far
+        )
+
+    def near_target(u):
+        index, row, column = units[u]
+        return outs[index].at[pl.ds(row + half, HALF), pl.ds(column, COLUMNS)]
+
+    def near_copy(u):
+        return remote(
+            mine.at[u % 5, z, x], near_target(u), s_near.at[u % 2], r_near.at[u], over_core
+        )
+
+    def near_arrival(u):
+        index, row, column = units[u]
+        target = outs[index].at[pl.ds(row + other_half, HALF), pl.ds(column, COLUMNS)]
+        return remote(
+            mine.at[u % 5, z, x], target, s_near.at[u % 2], r_near.at[u], over_core
+        )
+
+    def near_local(u):
+        return pltpu.make_async_copy(mine.at[u % 5, z, x], near_target(u), local.at[u % 2])
+
+    def add(into, other):
+        into[...] = (into[...].astype(F32) + other[...].astype(F32)).astype(BF16)
+
+    def stage0(u):
+        load_copy(u).start()
+        core_copy(u).start()
+
+    def stage1(u):
+        load_copy(u).wait()
+        core_copy(u).wait()
+
+        @pl.loop(0, 4)
+        def _(i):
+            add(mine.at[u % 5, i, 1 - x], core_in.at[u % 2, i, 1 - x])
+
+        x_copy(u).start()
+
+        @pl.loop(0, 4)
+        def _(i):
+            add(mine.at[u % 5, i, x], core_in.at[u % 2, i, x])
+
+    def stage2(u):
+        x_copy(u).wait()
+        for part, target_z in ((0, z_other), (1, 3 - z_other)):
+            add(mine.at[u % 5, target_z, x], x_in.at[u % 4, target_z])
+            z_copy(u, part).start()
+        for target_z in (z, 3 - z):
+            add(mine.at[u % 5, target_z, x], x_in.at[u % 4, target_z])
+
+    def stage3(u):
+        z_copy(u, 0).wait()
+        z_copy(u, 1).wait()
+        add(mine.at[u % 5, 3 - z, x], z_in.at[u % 4, 1])
+        far_copy(u).start()
+        add(mine.at[u % 5, z, x], z_in.at[u % 4, 0])
+
+        @pl.when(keeps)
+        def _():
+            near_local(u).start()
+
+        @pl.when(jnp.logical_not(keeps))
+        def _():
+            near_copy(u).start()
+
+    def stage4(u):
+        far_copy(u).wait_send()
+
+        @pl.when(keeps)
+        def _():
+            near_local(u).wait()
+            near_arrival(u).wait_recv()
+
+        @pl.when(jnp.logical_not(keeps))
+        def _():
+            near_copy(u).wait_send()
+
+    last = len(units)
+    order = ((stage1, 1), (stage0, 0), (stage2, 2), (stage3, 3), (stage4, 4))
+    for step in range(last + 4):
+        for stage, depth in order:
+            if 0 <= step - depth < last:
+                stage(step - depth)
+
+    @pl.when(jnp.logical_not(keeps))
+    def _():
+        for u in range(last):
+            far_arrival(u, 0).wait_recv()
+            far_arrival(u, 1).wait_recv()
+
+
+def scatter(grads, collective_id):
+    count = len(grads)
+    shapes = [(g.shape[0] // 8, g.shape[1]) for g in grads]
+    units = units_of(shapes)
+    dma = pltpu.SemaphoreType.DMA
+    return pl.pallas_call(
+        functools.partial(scatter_kernel, units, count),
+        out_shape=[jax.ShapeDtypeStruct(s, BF16) for s in shapes],
+        in_specs=[ANY] * count,
+        out_specs=[ANY] * count,
+        scratch_shapes=[
+            pltpu.VMEM((5, 4, 2, HALF, COLUMNS), BF16),
+            pltpu.VMEM((2, 4, 2, HALF, COLUMNS), BF16),
+            pltpu.VMEM((4, 4, HALF, COLUMNS), BF16),
+            pltpu.VMEM((4, 2, HALF, COLUMNS), BF16),
+            dma((2,)),
+            dma((2,)),
+            dma((2,)),
+            dma((4,)),
+            dma((4,)),
+            dma((4, 2)),
+            dma((4, 2)),
+            dma((2,)),
+            dma((len(units), 2)),
+            dma((2,)),
+            dma((len(units),)),
+            dma((2,)),
+        ],
+        compiler_params=pltpu.CompilerParams(
+            collective_id=collective_id, has_side_effects=True, vmem_limit_bytes=40 * 2**20
+        ),
+    )(*[g.reshape((4, 2) + s) for g, s in zip(grads, shapes)])
+
+
+def per_device(
+    frames_in,
+    noise,
+    lengths,
+    span_starts,
+    w_in1,
+    w_out1,
+    w_qkv,
+    w_attn,
+    w_point1,
+    w_point2,
+    w_in2,
+    w_out2,
+    norm_params,
+    kernel,
+    slopes,
+    cotangent,
+):
+    utterances, frames, width = frames_in.shape
+    heads = slopes.shape[0]
+    head_dim = width // heads
+    length = frames * 8
+    taps = kernel.shape[0]
+    half_taps = taps // 2
+    factor = head_dim ** (-0.5)
+    frame_pos = lax.axis_index("seq") * frames + jnp.arange(frames, dtype=jnp.int32)
+    span_begin = span_starts[:, :, None]
+    masked = jnp.any(
+        (span_begin <= frame_pos[None, None, :]) & (frame_pos[None, None, :] < span_begin + SPAN),
+        axis=1,
+    )
+    start = jnp.where(masked[..., None], noise, frames_in)
+    lens = jnp.broadcast_to(lengths.astype(F32)[:, None, None], (utterances, 8, 128))
+    start, cot, lens = exchange((start, cotangent, lens), True, 0)
+    h0 = start.reshape(length, width).astype(F32)
+    cot = cot.reshape(length, width).astype(F32)
+    live_count = lens[0, 0, 0]
+    position = jnp.arange(length, dtype=jnp.int32).astype(F32)
+    live = (position < live_count).astype(F32)[:, None]
+    key_live = position < live_count
+    gain, shift = norm_params[:, 0], norm_params[:, 1]
+    in1, out1, qkv, attn, point1, point2, in2, out2 = gather(
+        (w_in1, w_out1, w_qkv, w_attn, w_point1, w_point2, w_in2, w_out2), 1
+    )
+    a1 = layer_norm(h0, gain[0], shift[0]).astype(BF16)
+    u1 = matmul(a1, in1)
+    s1 = jax.nn.silu(u1).astype(BF16)
+    x1 = h0 + 0.5 * matmul(s1, out1)
+    a2 = layer_norm(x1, gain[1], shift[1]).astype(BF16)
+    packed = matmul(a2, qkv).astype(BF16).reshape(length, 3, heads, head_dim)
+    q, k, v = packed[:, 0], packed[:, 1], packed[:, 2]
+    distance = jnp.abs(position[:, None] - position[None, :]) / length
+    scores = jnp.einsum("qhd,khd->hqk", q, k, preferred_element_type=F32) * factor
+    scores = scores - slopes[:, None, None] * distance[None]
+    scores = jnp.where(key_live[None, None, :], scores, NEGATIVE)
+    top = jnp.max(scores, axis=-1, keepdims=True)
+    expd = jnp.exp(scores - top)
+    prob = expd / jnp.sum(expd, axis=-1, keepdims=True)
+    prob_low = prob.astype(BF16)
+    o = jnp.einsum("hqk,khd->qhd", prob_low, v, preferred_element_type=F32)
+    ob = o.astype(BF16).reshape(length, width)
+    x2 = x1 + matmul(ob, attn)
+    a3 = layer_norm(x2, gain[2], shift[2]).astype(BF16)
+    z = matmul(a3, point1)
+    g = glu_gate(z, live).astype(BF16)
+    padded = jnp.pad(g, ((half_taps, half_taps), (0, 0)))
+    depth = kernel[0] * padded[0:length].astype(F32)
+    for t in range(1, taps):
+        depth = depth + kernel[t] * padded[t : t + length].astype(F32)
+    c4 = swish_norm(depth, gain[3], shift[3]).astype(BF16)
+    x3 = x2 + matmul(c4, point2)
+    a5 = layer_norm(x3, gain[4], shift[4]).astype(BF16)
+    u2 = matmul(a5, in2)
+    s2 = jax.nn.silu(u2).astype(BF16)
+    x4 = x3 + 0.5 * matmul(s2, out2)
+    result = layer_norm(x4, gain[5], shift[5]).astype(BF16)
+    _, back = jax.vjp(layer_norm, x4, gain[5], shift[5])
+    dx4, gain5, shift5 = back(cot)
+    df2 = (0.5 * dx4).astype(BF16)
+    _, back = jax.vjp(jax.nn.silu, u2)
+    du2 = back(matmul_right_t(df2, out2))[0].astype(BF16)
+    _, back = jax.vjp(layer_norm, x3, gain[4], shift[4])
+    dn, gain4, shift4 = back(matmul_right_t(du2, in2))
+    dx3 = dx4 + dn
+    dc = dx3.astype(BF16)
+    _, back = jax.vjp(swish_norm, depth, gain[3], shift[3])
+    dd, gain3, shift3 = back(matmul_right_t(dc, point2))
+    dd = dd.astype(BF16)
+    dd_padded = jnp.pad(dd, ((half_taps, half_taps), (0, 0)))
+    dg = jnp.zeros((length, width), F32)
+    kernel_rows = []
+    for t in range(taps):
+        lower = 2 * half_taps - t
+        dg = dg + kernel[t] * dd_padded[lower : lower + length].astype(F32)
+        kernel_rows.append(jnp.sum(dd.astype(F32) * padded[t : t + length].astype(F32), axis=0))
+    _, back = jax.vjp(lambda joined: glu_gate(joined, live), z)
+    dz = back(dg)[0].astype(BF16)
+    _, back = jax.vjp(layer_norm, x2, gain[2], shift[2])
+    dn, gain2, shift2 = back(matmul_right_t(dz, point1))
+    dx2 = dx3 + dn
+    da = dx2.astype(BF16)
+    do = matmul_right_t(da, attn).astype(BF16).reshape(length, heads, head_dim)
+    delta = jnp.sum(do.astype(F32) * o, axis=-1)
+    dp = jnp.einsum("qhd,khd->hqk", do, v, preferred_element_type=F32)
+    ds_exact = prob * (dp - delta.T[..., None])
+    dslopes = -jnp.sum(ds_exact * distance[None], axis=(1, 2))
+    ds = ds_exact.astype(BF16)
+    dq = jnp.einsum("hqk,khd->qhd", ds, k, preferred_element_type=F32) * factor
+    dk = jnp.einsum("hqk,qhd->khd", ds, q, preferred_element_type=F32) * factor
+    dv = jnp.einsum("hqk,qhd->khd", prob_low, do, preferred_element_type=F32)
+    dqkv = jnp.stack([dq, dk, dv], axis=1).astype(BF16).reshape(length, 3 * width)
+    _, back = jax.vjp(layer_norm, x1, gain[1], shift[1])
+    dn, gain1, shift1 = back(matmul_right_t(dqkv, qkv))
+    dx1 = dx2 + dn
+    df1 = (0.5 * dx1).astype(BF16)
+    _, back = jax.vjp(jax.nn.silu, u1)
+    du1 = back(matmul_right_t(df1, out1))[0].astype(BF16)
+    _, back = jax.vjp(layer_norm, h0, gain[0], shift[0])
+    dn, gain0, shift0 = back(matmul_right_t(du1, in1))
+    dh0 = (dx1 + dn).astype(BF16)
+    pairs = (
+        (a1, du1),
+        (s1, df1),
+        (a2, dqkv),
+        (ob, da),
+        (a3, dz),
+        (c4, dc),
+        (a5, du2),
+        (s2, df2),
+    )
+    grads = scatter([matmul_left_t(a, b).astype(BF16) for a, b in pairs], 2)
+    small = jnp.concatenate(
+        [
+            jnp.stack([gain0, shift0, gain1, shift1, gain2, shift2, gain3, shift3, gain4, shift4, gain5, shift5]),
+            jnp.stack(kernel_rows),
+            jnp.pad(dslopes, (0, width - heads))[None],
+            jnp.zeros((14, width), F32),
+        ]
+    ).astype(BF16)
+    small = jnp.broadcast_to(small[None], (8,) + small.shape)
+    block_out, dframes, small = exchange(
+        (result.reshape(8, frames, width), dh0.reshape(8, frames, width), small), False, 3
+    )
+    small = jnp.sum(small.astype(F32), axis=0)
+    grad_frames = jnp.where(masked[..., None], 0.0, dframes.astype(F32))
+    return (
+        block_out,
+        grad_frames,
+        *[grad.astype(F32) for grad in grads],
+        small[:12].reshape(6, 2, width),
+        small[12:17],
+        small[17, :heads],
+    )
+
+
 def solution(mesh):
     in_specs = (
         P("dp", "seq", None),
@@ -410,6 +994,7 @@
         P("dp", None),
         P("dp"),
     )
+    grouped = mesh.shape["seq"] == 8 and mesh.shape["dp"] == 4
     return jax.shard_map(
-        per_device, mesh=mesh, in_specs=in_specs, out_specs=out_specs, check_vma=False
-    )
+        per_device if grouped else per_device_any, mesh=mesh, in_specs=in_specs, out_specs=out_specs, check_vma=False
+    )

time: 2190 us -> 872 us (0.40)
  waiting for transfers between devices: 1720 us -> 0 us
  Pallas kernels: 0 us -> 616 us
  blocking collectives: 97.6 us -> 0 us
  matrix products: 234 us -> 159 us
  local copies, waits for them, and re-layouts: 58.9 us -> 27 us
    all_gather x12 -> x0, waiting for transfers between devices: 1030 us -> none  [the longest x1 125 us: per_device(): lax.all_gather(shards[0], 'seq', axis=0, tiled=True)]
    reduce_scatter x2 -> x0, waiting for transfers between devices: 678 us -> none  [per_device(): lax.psum_scatter(jnp.concatenate([matmul_left_t(left_side, right_side) fo...]
    pallas_call x0 -> x4, Pallas kernels: none -> 616 us  [the longest x1 282 us: scatter(): pl.pallas_call(functools.partial(scatter_kernel, units, count), out_shape...]
    all_gather x2 -> x0, blocking collectives: 67 us -> none  [the longest x1 34.9 us: per_device(): lax.all_gather(log_total.astype(jnp.bfloat16), 'seq', axis=1, tiled=True)]
    dot_general x7 -> x6, matrix products: 63.3 us -> 14.7 us  [the longest x1 5.31 us: per_device(): dp = jnp.einsum('qhd,khd->hqk', do, v, preferred_element_type=F32)]
    psum x1 -> x0, blocking collectives: 30.6 us -> none  [per_device(): lax.psum(grad_norms.astype(jnp.bfloat16), 'seq').astype(jnp.float32)]
    dot_general x8, matrix products: 61.5 us -> 35.8 us  [matmul(): return jnp.dot(left_side, right_side, preferred_element_type=jnp.float32)]
  transfers between devices with their start and end apart: 18 -> 0, of which waited for: 16 -> 0; matrix products, arithmetic and copies ran while one was open for 11% -> 0% of each run, Pallas kernels for 0% -> 0%
where the time goes in v1:
time: 872 us; the launch traced here: 864 us
  Pallas kernels  616 us (71%)
  matrix products  159 us (18%)
  other arithmetic  59.9 us (7%)
  local copies, waits for them, and re-layouts  27 us (3%)
    pallas_call x1, Pallas kernels, scatter(): pl.pallas_call(functools.partial(scatter_kernel, units, count), out_shape...  282 us
    pallas_call x1, Pallas kernels, gather(): pl.pallas_call(functools.partial(gather_kernel, units, count), out_shape=...  220 us
    pallas_call x2, Pallas kernels, exchange(): pl.pallas_call(functools.partial(exchange_kernel, count, to_utterances),...  115 us
    dot_general x8, matrix products, matmul_left_t(): lax.dot_general(left_side, right_side, (((0,), (0,)), ((), ())), preferre...  54.2 us
    dot_general x8, matrix products, matmul_right_t(): lax.dot_general(left_side, right_side, (((1,), (1,)), ((), ())), preferre...  54 us
    dot_general x8, matrix products, matmul(): return jnp.dot(left_side, right_side, preferred_element_type=jnp.float32)  35.8 us

profile of v1, /device:TPU:1, one launch (start us, length us, event | category | flops | bytes accessed | tf_op | source)
XLA Modules:
  0.0 864.1 jit_solution(14215541726656075136)
XLA Ops:
  9.3 52.7 %shard_map.255 = (bf16[8,64,1024]{2,1,0:T(8,128)(2,1)}, bf16[8,64,1024]{2,1,0:T(8,128)(2,1)}, f32[8,8,128]{2,1,0:T(8,128)}) custom-call(bf16[8,64,1024]{2,1,0:T(8,128)(2,1)} %broadcast_select_fusion.refs_0_, bf16[8,64,1024]{2,1,0:T(8,128)(2,1)} %refs_1_.2, f32[8,8,128]{2,1,0:T(8,128)} %broadcast_in_dim.57.refs_2_), custom_call_target="tpu_custom_call" | custom-call | tf_op jit(solution)/shard_map/pallas_call | solution.py:510
  69.6 219.9 %shard_map.256 = (bf16[4,2,128,4096]{3,2,1,0:T(8,128)(2,1)}, bf16[4,2,512,1024]{3,2,1,0:T(8,128)(2,1)}, bf16[4,2,128,3072]{3,2,1,0:T(8,128)(2,1)}, bf16[4,2,128,...) custom-call(bf16[128,4096]{1,0:T(8,128)(2,1)} %refs_0_.1, ...), custom_call_target="tpu_custom_call" | custom-call | tf_op jit(solution)/shard_map/pallas_call | solution.py:603
  289.5 7.2 fusion.109
  296.8 4.7 fusion.104
  302.0 4.0 fusion.57
  310.6 8.4 fusion.105
  319.1 4.7 fusion.13
  340.5 7.0 fusion.91
  347.5 7.5 fusion.108
  359.0 12.8 %fusion.3 = bf16[512,4096]{1,0:T(8,128)(2,1)} fusion(f32[512,4096]{1,0:T(8,128)} %fusion.91, bf16[4096,1024]{1,0:T(8,128)(2,1)} %bitcast.220, f32[512,1024]{1,0:T(8,128)S(1)} %get-tuple-element.90, f32[512]{0:T(512)S(1)} %negate_multiply_fusion.5), kind=kOutput, calls=%fused_computation.5 | convolution fusion | flops 4317511680 | bytes 23070720 | tf_op jit(solution)/shard_map/dot_general | solution.py:56
  371.8 8.8 %multiply_reduce_fusion.1 = (bf16[1024]{0:T(1024)(128)(2,1)S(1)}, f32[512]{0:T(512)S(1)}, bf16[1024]{0:T(1024)(128)(2,1)S(1)}, f32[512,1024]{1,0:T(8,128)S(1)}) fusion(f32[512,1024]{1,0:T(8,128)S(1)} %get-tuple-element.131, f32[512]{0:T(512)S(1)} %fusion.78, f32[512]{0:T(512)S(1)} %broadcast_multiply_fusion.2, f32[1024]{0:T(1024)S(1)} %bitcast.186, ...), kind=kOutput, calls=%fused_computation.102 | convolution fusion | flops 4299159040 | bytes 16791552 | tf_op jit(solution)/shard_map/dot_general | solution.py:56
  380.5 11.3 %convolution_convert_fusion = bf16[4096,1024]{1,0:T(8,128)(2,1)} fusion(f32[512,1024]{1,0:T(8,128)S(1)} %get-tuple-element.90, f32[512]{0:T(512)S(1)} %negate_multiply_fusion.5, f32[512,4096]{1,0:T(8,128)} %fusion.91), kind=kOutput, calls=%fused_computation.17 | convolution fusion | flops 4311220224 | bytes 18876416 | tf_op jit(solution)/shard_map/dot_general | solution.py:62
  406.6 4.7 convolution_convert_fusion.6
  424.0 5.3 multiply_reduce_fusion
  434.0 4.2 multiply_reduce_fusion.4
  440.1 13.4 %fusion.6 = bf16[512,4096]{1,0:T(8,128)(2,1)} fusion(f32[512,4096]{1,0:T(8,128)} %copy-done.58, bf16[4096,1024]{1,0:T(8,128)(2,1)} %bitcast.214, f32[512,1024]{1,0:T(8,128)S(1)} %add_add_fusion.6), kind=kOutput, calls=%fused_computation.8 | convolution fusion | flops 4316987392 | bytes 23068672 | tf_op jit(solution)/shard_map/dot_general | solution.py:56
  453.6 7.4 fusion.93
  463.6 10.9 %convolution_convert_fusion.2 = bf16[4096,1024]{1,0:T(8,128)(2,1)} fusion(f32[512,1024]{1,0:T(8,128)S(1)} %add_add_fusion.6, f32[512,4096]{1,0:T(8,128)} %copy-done.58), kind=kOutput, calls=%fused_computation.19 | convolution fusion | flops 4310695936 | bytes 18874368 | tf_op jit(solution)/shard_map/dot_general | solution.py:62
  476.1 4.5 fusion.47
  481.4 62.0 %shard_map.257 = (bf16[8,64,1024]{2,1,0:T(8,128)(2,1)}, bf16[8,64,1024]{2,1,0:T(8,128)(2,1)}, bf16[8,32,1024]{2,1,0:T(8,128)(2,1)}) custom-call(bf16[8,64,1024]{2,1,0:T(8,128)(2,1)} %bitcast.159, bf16[8,64,1024]{2,1,0:T(8,128)(2,1)} %bitcast.158, bf16[8,32,1024]{2,1,0:T(8,128)(2,1)} %broadcast_in_dim.73.refs_2_), custom_call_target="tpu_custom_call" | custom-call | tf_op jit(solution)/shard_map/pallas_call | solution.py:510
  546.4 9.1 %convolution_convert_fusion.4 = bf16[1024,3072]{1,0:T(8,128)(2,1)} fusion(bf16[512,3072]{0,1:T(8,128)(2,1)} %bitcast.161, f32[512,1024]{1,0:T(8,128)} %copy-done.12, f32[1024]{0:T(1024)S(1)} %bitcast.204, f32[1024]{0:T(1024)S(1)} %bitcast.192, f32[512]{0:T(512)S(1)} %copy-done.44, f32[512]{0:T(512)S(1)} %copy-done.35), kind=kOutput, calls=%fused_computation.22 | convolution fusion | flops 3226992640 | bytes 11546624 | tf_op jit(solution)/shard_map/dot_general | solution.py:62
  555.5 7.2 convolution_convert_fusion.1
  564.3 6.7 convolution_convert_fusion.3
  571.0 281.6 %shard_map.258 = (bf16[128,4096]{1,0:T(8,128)(2,1)S(1)}, bf16[512,1024]{1,0:T(8,128)(2,1)S(1)}, bf16[128,3072]{1,0:T(8,128)(2,1)S(1)}, bf16[128,1024]{1,0:T(8,12...) custom-call(bf16[4,2,128,4096]{3,2,1,0:T(8,128)(2,1)} %bitcast.156, ...), custom_call_target="tpu_custom_call" | custom-call | tf_op jit(solution)/shard_map/pallas_call | solution.py:779
  (265 shorter events, 95.9 us)
Async XLA Ops:
  5.4 63.8 %copy-start.29 = (f32[1,1,1024]{2,1,0:T(1,128)}, f32[1,1,1024]{2,1,0:T(1,128)S(1)}, u32[]{:S(2)}) copy-start(f32[1,1,1024]{2,1,0:T(1,128)S(1)} %get-tuple-element.111) | copy-start | bytes 12292
  5.4 63.8 %copy-start.31 = (f32[1,1,1024]{2,1,0:T(1,128)}, f32[1,1,1024]{2,1,0:T(1,128)S(1)}, u32[]{:S(2)}) copy-start(f32[1,1,1024]{2,1,0:T(1,128)S(1)} %get-tuple-element.110) | copy-start | bytes 12292
  5.4 296.5 %copy-start.39 = (f32[1,1,1024]{2,1,0:T(1,128)}, f32[1,1,1024]{2,1,0:T(1,128)S(1)}, u32[]{:S(2)}) copy-start(f32[1,1,1024]{2,1,0:T(1,128)S(1)} %get-tuple-element.109) | copy-start | bytes 12292
  5.4 296.5 %copy-start.48 = (f32[1,1,1024]{2,1,0:T(1,128)}, f32[1,1,1024]{2,1,0:T(1,128)S(1)}, u32[]{:S(2)}) copy-start(f32[1,1,1024]{2,1,0:T(1,128)S(1)} %get-tuple-element.108) | copy-start | bytes 12292
  5.4 332.9 %copy-start.46 = (f32[1,1,1024]{2,1,0:T(1,128)}, f32[1,1,1024]{2,1,0:T(1,128)S(1)}, u32[]{:S(2)}) copy-start(f32[1,1,1024]{2,1,0:T(1,128)S(1)} %get-tuple-element.102) | copy-start | bytes 12292
  289.5 12.4 %slice-start.6 = ((s8[6291456]{0:T(1024)(128)(4,1)}), s8[4194304]{0:T(1024)(128)(4,1)S(1)}, s32[]{:S(2)}) async-start(s8[6291456]{0:T(1024)(128)(4,1)} %bitcast.224), calls=%async_computation.6 | async-start | bytes 8388608
  336.3 11.2 %slice-start.4 = ((s8[8388608]{0:T(1024)(128)(4,1)}), s8[4194304]{0:T(1024)(128)(4,1)S(1)}, s32[]{:S(2)}) async-start(s8[8388608]{0:T(1024)(128)(4,1)} %bitcast.221), calls=%async_computation.4 | async-start | bytes 8388608
  337.9 54.0 %copy-start.15 = (f32[512,1024]{1,0:T(8,128)}, f32[512,1024]{1,0:T(8,128)S(1)}, u32[]{:S(2)}) copy-start(f32[512,1024]{1,0:T(8,128)S(1)} %get-tuple-element.131) | copy-start | bytes 6291460
  337.9 9.5 %slice-start.5 = ((s8[8388608]{0:T(1024)(128)(4,1)}), s8[4194304]{0:T(1024)(128)(4,1)S(1)}, s32[]{:S(2)}) async-start(s8[8388608]{0:T(1024)(128)(4,1)} %bitcast.221), calls=%async_computation.5 | async-start | bytes 8388608
  439.8 13.7 %slice-start = ((s8[8388608]{0:T(1024)(128)(4,1)}), s8[4194304]{0:T(1024)(128)(4,1)S(1)}, s32[]{:S(2)}) async-start(s8[8388608]{0:T(1024)(128)(4,1)} %bitcast.211), calls=%async_computation | async-start | bytes 8388608
  440.1 23.5 %copy-start.10 = (f32[512,1024]{1,0:T(8,128)}, f32[512,1024]{1,0:T(8,128)S(1)}, u32[]{:S(2)}) copy-start(f32[512,1024]{1,0:T(8,128)S(1)} %add_add_fusion.6) | copy-start | bytes 6291460
  440.1 13.4 %copy-start.4 = (bf16[8,64,1024]{2,1,0:T(8,128)(2,1)S(1)}, bf16[8,64,1024]{2,1,0:T(8,128)(2,1)}, u32[]{:S(2)}) copy-start(bf16[8,64,1024]{2,1,0:T(8,128)(2,1)} %get-tuple-element.35) | copy-start | bytes 3145732
  440.1 13.4 %copy-start.30 = (f32[1,1,1024]{2,1,0:T(1,128)S(1)}, f32[1,1,1024]{2,1,0:T(1,128)}, u32[]{:S(2)}) copy-start(f32[1,1,1024]{2,1,0:T(1,128)} %copy-done.29) | copy-start | bytes 12292
  440.1 13.4 %copy-start.33 = (f32[512]{0:T(512)S(1)}, f32[512]{0:T(512)}, u32[]{:S(2)}) copy-start(f32[512]{0:T(512)} %div.193) | copy-start | bytes 6148
  440.1 13.4 %slice-start.1 = ((s8[8388608]{0:T(1024)(128)(4,1)}), s8[4194304]{0:T(1024)(128)(4,1)S(1)}, s32[]{:S(2)}) async-start(s8[8388608]{0:T(1024)(128)(4,1)} %bitcast.211), calls=%async_computation.1 | async-start | bytes 8388608
  453.6 7.4 copy-start.28
  461.0 13.7 %copy-start.11 = (f32[512,1024]{1,0:T(8,128)}, f32[512,1024]{1,0:T(8,128)S(1)}, u32[]{:S(2)}) copy-start(f32[512,1024]{1,0:T(8,128)S(1)} %get-tuple-element.138) | copy-start | bytes 6291460
  463.5 11.0 %copy-start.45 = (f32[512]{0:T(512)S(1)}, f32[512]{0:T(512)}, u32[]{:S(2)}) copy-start(f32[512]{0:T(512)} %add.281) | copy-start | bytes 6148
  480.5 65.8 %copy-start.49 = (f32[1,1,1024]{2,1,0:T(1,128)S(1)}, f32[1,1,1024]{2,1,0:T(1,128)}, u32[]{:S(2)}) copy-start(f32[1,1,1024]{2,1,0:T(1,128)} %copy-done.48) | copy-start | bytes 12292
  546.4 9.1 %copy-start.16 = (f32[512,1024]{1,0:T(8,128)S(1)}, f32[512,1024]{1,0:T(8,128)}, u32[]{:S(2)}) copy-start(f32[512,1024]{1,0:T(8,128)} %copy-done.15) | copy-start | bytes 6291460
  546.4 9.1 %copy-start.47 = (f32[1,1,1024]{2,1,0:T(1,128)S(1)}, f32[1,1,1024]{2,1,0:T(1,128)}, u32[]{:S(2)}) copy-start(f32[1,1,1024]{2,1,0:T(1,128)} %copy-done.46) | copy-start | bytes 12292
  546.4 9.1 %copy-start.60 = (bf16[512,4096]{1,0:T(8,128)(2,1)S(1)}, bf16[512,4096]{1,0:T(8,128)(2,1)}, u32[]{:S(2)}) copy-start(bf16[512,4096]{1,0:T(8,128)(2,1)} %fusion.3) | copy-start | bytes 12582916
  555.5 7.3 copy-start.26
  555.5 8.8 %copy-start.59 = (bf16[512,4096]{1,0:T(8,128)(2,1)S(1)}, bf16[512,4096]{1,0:T(8,128)(2,1)}, u32[]{:S(2)}) copy-start(bf16[512,4096]{1,0:T(8,128)(2,1)} %fusion.6) | copy-start | bytes 12582916
  (47 other events, 161.3 us)

commit v2 on v1

--- a/solution.py
+++ b/solution.py
@@ -533,6 +533,7 @@
 ROWS = 128
 HALF = 64
 COLUMNS = 1024
+LAGS = (0, 1, 2, 3, 5, 7, 8)
 SPLIT = 384
 
 
@@ -571,8 +572,9 @@
 
     def third(u):
         _, full, rows, _, part, _ = spot(units[u])
-        piece = full.at[:, :, rows, part]
-        return [remote(piece, piece, send.at[u, 4], recv.at[u, 4], over_y)]
+        pieces = [full.at[:, 1 - x, rows, part]] + [full.at[other, x, rows, part] for other in zs]
+        out = [remote(p, p, send.at[u, 4 + j], recv.at[u, 4 + j], over_y) for j, p in enumerate(pieces)]
+        return out
 
     def fourth(u):
         _, full, rows, _, _, whole = spot(units[u])
@@ -805,6 +807,478 @@
     )(*[g.reshape((4, 2) + s) for g, s in zip(grads, shapes)])
 
 
+def blocks(rows, size):
+    def run(body):
+        @pl.loop(0, rows // size)
+        def _(i):
+            body(pl.ds(pl.multiple_of(i * size, size), size))
+
+    return run
+
+
+def normalise(v, norm, i):
+    average = jnp.mean(v, axis=-1, keepdims=True)
+    centred = v - average
+    variance = jnp.mean(centred * centred, axis=-1, keepdims=True)
+    return centred * lax.rsqrt(variance + EPSILON) * norm[i, 0:1, :] + norm[i, 1:2, :]
+
+
+TILE = 256
+
+
+def sigmoid(v):
+    return 0.5 * jnp.tanh(0.5 * v) + 0.5
+
+
+def silu(v):
+    return v * sigmoid(v)
+
+
+def times_unit(left, weight, emit, poll):
+    unit, loads = weight
+    for n in range(COLUMNS // TILE):
+        columns = pl.ds(n * TILE, TILE)
+        loads[n].wait()
+        emit(columns, jnp.dot(left[...], unit[:, :, :, columns].reshape(COLUMNS, TILE), preferred_element_type=F32))
+        poll()
+
+
+def score_block(q, k, slope_row, first, live_keys):
+    shape = (q.shape[0], k.shape[0])
+    scores = lax.dot_general(q, k, (((1,), (1,)), ((), ())), preferred_element_type=F32)
+    rows = lax.broadcasted_iota(jnp.int32, shape, 0) + first
+    keys = lax.broadcasted_iota(jnp.int32, shape, 1)
+    distance = jnp.abs(rows - keys).astype(F32) * (1.0 / k.shape[0])
+    scores = scores * (q.shape[1] ** -0.5) - slope_row * distance
+    return jnp.where(keys.astype(F32) < live_keys, scores, NEGATIVE), distance
+
+
+def softmax_block(scores):
+    top = jnp.max(scores, axis=-1, keepdims=True)
+    expd = jnp.exp(scores - top)
+    return expd / jnp.sum(expd, axis=-1, keepdims=True)
+
+
+QUERIES = 128
+BLOCK = 32
+
+
+def forward_kernel(units, names, *refs):
+    r = dict(zip(names, refs))
+    norm, taps, slope = r["norm"], r["taps"], r["slope"]
+    length, width = r["x"].shape[1:]
+    heads = slope.shape[0]
+    head_dim = width // heads
+    z, x, y, core = place()
+    seq, group = z * 2 + x, z // 2
+    utterance = utterance_of(z, x, core)
+    same = group == core
+    zs = z_partners(z)
+    over_z = [device(other, x, y, core) for other in zs]
+    over_x = device(z, 1 - x, y, core)
+    over_y = device(z, x, 1 - y, core)
+    over_core = device(z, x, y, 1 - core)
+    mates = [utterance_in_round(seq, i) for i in range(8)]
+    givers = [device(s // 2, lax.rem(s, 2), y, group) for s in [seq_in_round(utterance, i) for i in range(8)]]
+    targets = [home_of(u, y, core) for u in mates]
+    barrier = pltpu.get_barrier_semaphore()
+
+    @pl.when(jnp.logical_not(same))
+    def _():
+        pl.semaphore_signal(barrier, inc=1, device_id=givers[0], device_id_type=MESH)
+
+    for partner in givers[1:] + [over_z[0], over_z[2], over_x, over_y, over_core]:
+        pl.semaphore_signal(barrier, inc=1, device_id=partner, device_id_type=MESH)
+    pl.semaphore_wait(barrier, jnp.where(same, 12, 13))
+
+    swaps = (("start", "h0"), ("lens", "lens_here"), ("cot", "cot_out"))
+
+    def swap(i, j):
+        source, target = r[swaps[i][0]], r[swaps[i][1]]
+        return remote(source.at[mates[j]], target.at[seq], r["swap_send"].at[i, j], r["swap_recv"].at[i, j], targets[j])
+
+    def swap_local(i):
+        source, target = r[swaps[i][0]], r[swaps[i][1]]
+        return pltpu.make_async_copy(source.at[mates[0]], target.at[seq], r["swap_own"].at[i])
+
+    def swap_start(i, j):
+        if j > 0:
+            swap(i, j).start()
+            return
+
+        @pl.when(jnp.logical_not(same))
+        def _():
+            swap(i, 0).start()
+
+        @pl.when(same)
+        def _():
+            swap_local(i).start()
+
+    def swap_wait(i):
+        @pl.when(jnp.logical_not(same))
+        def _():
+            swap(i, 0).wait()
+
+        @pl.when(same)
+        def _():
+            swap_local(i).wait()
+
+        for j in range(1, 8):
+            swap(i, j).wait()
+
+    send, recv, own = r["send"], r["recv"], r["own"]
+    shards, fulls = r["shards"], r["fulls"]
+
+    def spot(unit):
+        index, row, column = unit
+        rows = pl.ds(row + pl.multiple_of(core * HALF, HALF), HALF)
+        mine = pl.ds(column + pl.multiple_of(y * SPLIT, 128), COLUMNS - SPLIT)
+        third = pl.ds(column + pl.multiple_of(y * (COLUMNS - SPLIT), 128), SPLIT)
+        return shards[index], fulls[index], rows, mine, third, pl.ds(column, COLUMNS)
+
+    middle = (z == 1) | (z == 2)
+    near_pair, far_pair = pl.ds(2 * (z // 2), 2), pl.ds(2 - 2 * (z // 2), 2)
+
+    class Along:
+        def __init__(self, copy, sends, gets):
+            self.copy, self.sends, self.gets = copy, sends, gets
+
+        def start(self):
+            @pl.when(self.sends)
+            def _():
+                self.copy.start()
+
+        def wait(self):
+            @pl.when(self.sends)
+            def _():
+                self.copy.wait_send()
+
+            @pl.when(self.gets)
+            def _():
+                self.copy.wait_recv()
+
+    def first(u):
+        shard, full, rows, mine, _, _ = spot(units[u])
+        every = pl.ds(units[u][2], COLUMNS)
+        return [
+            remote(shard.at[rows, mine], full.at[z, x, rows, mine], send.at[u, 0], recv.at[u, 0], over_z[0]),
+            pltpu.make_async_copy(shard.at[rows, every], full.at[z, x, rows, every], own.at[u]),
+        ]
+
+    def across(u):
+        _, full, rows, mine, _, _ = spot(units[u])
+        piece = full.at[near_pair, x, rows, mine]
+        return [Along(remote(piece, piece, send.at[u, 1], recv.at[u, 1], over_z[2]), middle, middle)]
+
+    def outward(u):
+        _, full, rows, mine, _, _ = spot(units[u])
+        piece = full.at[far_pair, x, rows, mine]
+        copy = remote(piece, piece, send.at[u, 2], recv.at[u, 2], over_z[0])
+        return [Along(copy, middle, jnp.logical_not(middle))]
+
+    def second(u):
+        _, full, rows, mine, _, _ = spot(units[u])
+        piece = full.at[:, x, rows, mine]
+        return [remote(piece, piece, send.at[u, 3], recv.at[u, 3], over_x)]
+
+    def third(u):
+        _, full, rows, _, part, _ = spot(units[u])
+        pieces = [full.at[:, 1 - x, rows, part]] + [full.at[other, x, rows, part] for other in zs]
+        out = [remote(p, p, send.at[u, 4 + j], recv.at[u, 4 + j], over_y) for j, p in enumerate(pieces)]
+        return out
+
+    def fourth(u):
+        _, full, rows, _, _, whole = spot(units[u])
+        piece = full.at[:, :, rows, whole]
+        return [remote(piece, piece, send.at[u, 8], recv.at[u, 8], over_core)]
+
+    stages = (first, across, outward, second, third, fourth)
+    last = len(units)
+    done = [0]
+
+    actions = []
+    ends = {}
+
+    def move(u, depth):
+        def act_on():
+            if depth > 0:
+                for copy in stages[depth - 1](u):
+                    copy.wait()
+            if depth < len(stages):
+                for copy in stages[depth](u):
+                    copy.start()
+
+        return act_on
+
+    for step in range(last + LAGS[-1]):
+        for depth, lag in enumerate(LAGS):
+            if 0 <= step - lag < last:
+                actions.append(move(step - lag, depth))
+                if depth == len(stages):
+                    ends[step - lag] = len(actions)
+        if 12 <= step < 20:
+            actions.append(functools.partial(swap_start, 2, step - 12))
+
+    def poll(count=1):
+        for _ in range(count):
+            if done[0] < len(actions):
+                actions[done[0]]()
+                done[0] += 1
+
+    taken = [0]
+
+    def weight():
+        u = taken[0]
+        taken[0] += 1
+        while done[0] < ends[u]:
+            poll()
+        index, row, column = units[u]
+        loads = []
+        for n in range(COLUMNS // TILE):
+            source = fulls[index].at[:, :, pl.ds(row, ROWS), pl.ds(column + n * TILE, TILE)]
+            target = r["unit"].at[u % 2, :, :, :, pl.ds(n * TILE, TILE)]
+            copy = pltpu.make_async_copy(source, target, r["load"].at[u % 2, n])
+            copy.start()
+            loads.append(copy)
+        return r["unit"].at[u % 2], loads
+
+    kept = []
+
+    def keep(source, target):
+        copy = pltpu.make_async_copy(source, target, r["kept"].at[len(kept)])
+        copy.start()
+        kept.append(copy)
+
+    xs, act, acc = r["x"], r["act"], r["acc"]
+    poll()
+    for j in range(8):
+        swap_start(0, j)
+    for j in range(8):
+        swap_start(1, j)
+    poll(4)
+    swap_wait(0)
+
+    @blocks(length, BLOCK)
+    def _(rows):
+        xs[0, rows, :] = r["h0"][rows.start // 64, pl.ds(pl.multiple_of(lax.rem(rows.start, 64), BLOCK), BLOCK), :].astype(F32)
+        act[rows, :] = normalise(xs[0, rows, :], norm, 0).astype(BF16)
+
+    keep(r["h0"], r["h0_out"])
+
+    def feed_forward(x_in, x_out, up, up_out):
+        hidden = r["hidden"]
+        for p in range(4):
+            unit, loads = weight()
+
+            for n in range(COLUMNS // TILE):
+                columns = pl.ds(n * TILE, TILE)
+                loads[n].wait()
+                value = jnp.dot(act[...], unit[:, :, :, columns].reshape(COLUMNS, TILE), preferred_element_type=F32)
+                up[p, :, columns] = value.astype(BF16)
+                value = silu(value).astype(BF16)
+                for t in range(2 * n, 2 * n + 2):
+                    place_at = pl.ds((2 * p + t // 4) * 128, 128)
+                    hidden[t % 4, :, place_at] = value[:, (t - 2 * n) * 128 : (t - 2 * n + 1) * 128]
+                poll()
+
+            keep(up.at[p], up_out.at[:, pl.ds(p * COLUMNS, COLUMNS)])
+        for q in range(4):
+            def emit(columns, value, q=q):
+                if q == 0:
+                    acc[:, columns] = value
+                else:
+                    acc[:, columns] = acc[:, columns] + value
+
+            times_unit(hidden.at[q], weight(), emit, poll)
+
+        @blocks(length, BLOCK)
+        def _(rows):
+            xs[x_out, rows, :] = xs[x_in, rows, :] + 0.5 * acc[rows, :]
+
+    feed_forward(0, 1, r["up"], r["u1_out"])
+    keep(xs.at[1], r["x1_out"])
+
+    @blocks(length, BLOCK)
+    def _(rows):
+        act[rows, :] = normalise(xs[1, rows, :], norm, 1).astype(BF16)
+
+    qkv = r["qkv"]
+    for i in range(3):
+
+        def emit(columns, value, i=i):
+            qkv[i, :, columns] = value.astype(BF16)
+
+        times_unit(act, weight(), emit, poll)
+    keep(qkv, r["qkv_out"])
+    swap_wait(1)
+    live_count = r["lens_here"][0, 0:1, 0:1]
+    keep(r["lens_here"], r["lens_out"])
+    attended = r["attended"]
+    for h in range(heads):
+        columns = pl.ds(h * head_dim, head_dim)
+
+        @blocks(length, QUERIES)
+        def _(rows, h=h, columns=columns):
+            scores, _ = score_block(
+                qkv[0, rows, columns], qkv[1, :, columns], slope[h : h + 1, :], rows.start, live_count
+            )
+            prob = softmax_block(scores).astype(BF16)
+            attended[rows, columns] = jnp.dot(prob, qkv[2, :, columns], preferred_element_type=F32).astype(BF16)
+
+        poll(2)
+    keep(attended, r["attended_out"])
+
+    def add_to(x_in, x_out):
+        def emit(columns, value):
+            xs[x_out, :, columns] = xs[x_in, :, columns] + value
+
+        return emit
+
+    times_unit(attended, weight(), add_to(1, 2), poll)
+    keep(xs.at[2], r["x2_out"])
+
+    @blocks(length, BLOCK)
+    def _(rows):
+        act[rows, :] = normalise(xs[2, rows, :], norm, 2).astype(BF16)
+
+    gates, gated = r["gates"], r["gated"]
+
+    def emit(columns, value):
+        acc[:, columns] = value
+        gates[0, :, columns] = value.astype(BF16)
+
+    times_unit(act, weight(), emit, poll)
+    gated[0:8, :] = jnp.zeros((8, width), F32)
+    gated[length + 8 : length + 16, :] = jnp.zeros((8, width), F32)
+
+    def emit(columns, value):
+        gates[1, :, columns] = value.astype(BF16)
+        live = lax.broadcasted_iota(jnp.int32, value.shape, 0).astype(F32) < live_count
+        passed = jnp.where(live, acc[:, columns] * sigmoid(value), 0.0)
+        gated[pl.ds(8, length), columns] = passed.astype(BF16).astype(F32)
+
+    times_unit(act, weight(), emit, poll)
+    keep(gates, r["gates_out"])
+    keep(gated, r["gated_out"])
+    depth = r["depth"]
+
+    @blocks(length, BLOCK)
+    def _(rows):
+        near = gated[pl.ds(pl.multiple_of(rows.start, BLOCK), BLOCK + 16), :]
+        total = taps[0:1, :] * near[6 : 6 + BLOCK]
+        for t in range(1, taps.shape[0]):
+            total = total + taps[t : t + 1, :] * near[6 + t : 6 + t + BLOCK]
+        depth[rows, :] = total
+        value = normalise(total, norm, 3)
+        act[rows, :] = (silu(value)).astype(BF16)
+
+    keep(depth, r["depth_out"])
+    times_unit(act, weight(), add_to(2, 3), poll)
+    keep(xs.at[3], r["x3_out"])
+
+    @blocks(length, BLOCK)
+    def _(rows):
+        act[rows, :] = normalise(xs[3, rows, :], norm, 4).astype(BF16)
+
+    feed_forward(3, 4, r["up2"], r["u2_out"])
+    keep(xs.at[4], r["x4_out"])
+
+    @blocks(length, BLOCK)
+    def _(rows):
+        act[rows, :] = normalise(xs[4, rows, :], norm, 5).astype(BF16)
+
+    keep(act, r["result_out"])
+    swap_wait(2)
+    for copy in kept:
+        copy.wait()
+
+
+def forward(start, lens, cot, norm, taps, slope, shards, collective_id):
+    shapes = [s.shape for s in shards]
+    units = units_of(shapes)
+    width = norm.shape[-1]
+    frames = start.shape[1]
+    length = 8 * frames
+    count = len(shards)
+    dma = pltpu.SemaphoreType.DMA
+    hidden = shapes[0][1]
+    wide = lambda *lead: jax.ShapeDtypeStruct(lead + (length, width), F32)
+    low = lambda *lead: jax.ShapeDtypeStruct(lead + (length, width), BF16)
+    up = jax.ShapeDtypeStruct((length, hidden), BF16)
+    outs = {
+        "cot_out": jax.ShapeDtypeStruct(cot.shape, cot.dtype),
+        "h0_out": jax.ShapeDtypeStruct(start.shape, start.dtype),
+        "u1_out": up,
+        "x1_out": wide(),
+        "qkv_out": low(3),
+        "attended_out": low(),
+        "x2_out": wide(),
+        "gates_out": low(2),
+        "gated_out": jax.ShapeDtypeStruct((length + 16, width), F32),
+        "depth_out": wide(),
+        "x3_out": wide(),
+        "u2_out": up,
+        "x4_out": wide(),
+        "result_out": low(),
+        "lens_out": jax.ShapeDtypeStruct(lens.shape, lens.dtype),
+    }
+    scratch = {
+        "h0": pltpu.VMEM(start.shape, BF16),
+        "lens_here": pltpu.VMEM(lens.shape, F32),
+        "x": pltpu.VMEM((5, length, width), F32),
+        "act": pltpu.VMEM((length, width), BF16),
+        "acc": pltpu.VMEM((length, width), F32),
+        "hidden": pltpu.VMEM((4, length, width), BF16),
+        "up": pltpu.VMEM((4, length, width), BF16),
+        "up2": pltpu.VMEM((4, length, width), BF16),
+        "qkv": pltpu.VMEM((3, length, width), BF16),
+        "attended": pltpu.VMEM((length, width), BF16),
+        "gates": pltpu.VMEM((2, length, width), BF16),
+        "gated": pltpu.VMEM((length + 16, width), F32),
+        "depth": pltpu.VMEM((length, width), F32),
+        "unit": pltpu.VMEM((2, 4, 2, ROWS, COLUMNS), BF16),
+        "load": dma((2, COLUMNS // TILE)),
+        "swap_send": dma((3, 8)),
+        "swap_recv": dma((3, 8)),
+        "swap_own": dma((3,)),
+        "send": dma((len(units), 9)),
+        "recv": dma((len(units), 9)),
+        "own": dma((len(units),)),
+        "kept": dma((32,)),
+    }
+    names = ["start", "lens", "cot", "norm", "taps", "slope"]
+    vmem = pl.BlockSpec(memory_space=pltpu.VMEM)
+
+    def body(*refs):
+        plain, rest = refs[:6], refs[6:]
+        ours, rest = rest[:count], rest[count:]
+        made, rest = rest[: len(outs)], rest[len(outs) :]
+        fulls, rest = rest[:count], rest[count:]
+        forward_kernel(
+            units,
+            names + list(outs) + list(scratch) + ["shards", "fulls"],
+            *plain,
+            *made,
+            *rest,
+            ours,
+            fulls,
+        )
+
+    results = pl.pallas_call(
+        body,
+        out_shape=list(outs.values()) + [jax.ShapeDtypeStruct((4, 2) + s, BF16) for s in shapes],
+        in_specs=[ANY, ANY, ANY, vmem, vmem, vmem] + [ANY] * count,
+        out_specs=[ANY] * (len(outs) + count),
+        scratch_shapes=list(scratch.values()),
+        compiler_params=pltpu.CompilerParams(
+            collective_id=collective_id, has_side_effects=True, vmem_limit_bytes=60 * 2**20
+        ),
+    )(start, lens, cot, norm, taps, slope, *shards)
+    made = dict(zip(outs, results[: len(outs)]))
+    fulls = [f.reshape(8 * s[0], s[1]) for f, s in zip(results[len(outs) :], shapes)]
+    return made, fulls
+
+
 def per_device(
     frames_in,
     noise,
@@ -838,24 +1312,27 @@
     )
     start = jnp.where(masked[..., None], noise, frames_in)
     lens = jnp.broadcast_to(lengths.astype(F32)[:, None, None], (utterances, 8, 128))
-    start, cot, lens = exchange((start, cotangent, lens), True, 0)
-    h0 = start.reshape(length, width).astype(F32)
-    cot = cot.reshape(length, width).astype(F32)
-    live_count = lens[0, 0, 0]
+    slope_rows = jnp.broadcast_to(slopes[:, None], (heads, length))
+    shards = (w_in1, w_out1, w_qkv, w_attn, w_point1, w_point2, w_in2, w_out2)
+    made, fulls = forward(start, lens, cotangent, norm_params, kernel, slope_rows, shards, 0)
+    in1, out1, qkv, attn, point1, point2, in2, out2 = fulls
+    gain, shift = norm_params[:, 0], norm_params[:, 1]
+    h0 = made["h0_out"].reshape(length, width).astype(F32)
+    cot = made["cot_out"].reshape(length, width).astype(F32)
+    live_count = made["lens_out"][0, 0, 0]
     position = jnp.arange(length, dtype=jnp.int32).astype(F32)
     live = (position < live_count).astype(F32)[:, None]
     key_live = position < live_count
-    gain, shift = norm_params[:, 0], norm_params[:, 1]
-    in1, out1, qkv, attn, point1, point2, in2, out2 = gather(
-        (w_in1, w_out1, w_qkv, w_attn, w_point1, w_point2, w_in2, w_out2), 1
-    )
+    u1, x1, x2, x3, u2, x4 = [made[n + "_out"].astype(F32) for n in ("u1", "x1", "x2", "x3", "u2", "x4")]
+    depth, result = made["depth_out"], made["result_out"]
     a1 = layer_norm(h0, gain[0], shift[0]).astype(BF16)
-    u1 = matmul(a1, in1)
     s1 = jax.nn.silu(u1).astype(BF16)
-    x1 = h0 + 0.5 * matmul(s1, out1)
     a2 = layer_norm(x1, gain[1], shift[1]).astype(BF16)
-    packed = matmul(a2, qkv).astype(BF16).reshape(length, 3, heads, head_dim)
-    q, k, v = packed[:, 0], packed[:, 1], packed[:, 2]
+    a3 = layer_norm(x2, gain[2], shift[2]).astype(BF16)
+    c4 = swish_norm(depth, gain[3], shift[3]).astype(BF16)
+    a5 = layer_norm(x3, gain[4], shift[4]).astype(BF16)
+    s2 = jax.nn.silu(u2).astype(BF16)
+    q, k, v = [p.reshape(length, heads, head_dim) for p in made["qkv_out"]]
     distance = jnp.abs(position[:, None] - position[None, :]) / length
     scores = jnp.einsum("qhd,khd->hqk", q, k, preferred_element_type=F32) * factor
     scores = scores - slopes[:, None, None] * distance[None]
@@ -864,23 +1341,10 @@
     expd = jnp.exp(scores - top)
     prob = expd / jnp.sum(expd, axis=-1, keepdims=True)
     prob_low = prob.astype(BF16)
-    o = jnp.einsum("hqk,khd->qhd", prob_low, v, preferred_element_type=F32)
-    ob = o.astype(BF16).reshape(length, width)
-    x2 = x1 + matmul(ob, attn)
-    a3 = layer_norm(x2, gain[2], shift[2]).astype(BF16)
-    z = matmul(a3, point1)
-    g = glu_gate(z, live).astype(BF16)
-    padded = jnp.pad(g, ((half_taps, half_taps), (0, 0)))
-    depth = kernel[0] * padded[0:length].astype(F32)
-    for t in range(1, taps):
-        depth = depth + kernel[t] * padded[t : t + length].astype(F32)
-    c4 = swish_norm(depth, gain[3], shift[3]).astype(BF16)
-    x3 = x2 + matmul(c4, point2)
-    a5 = layer_norm(x3, gain[4], shift[4]).astype(BF16)
-    u2 = matmul(a5, in2)
-    s2 = jax.nn.silu(u2).astype(BF16)
-    x4 = x3 + 0.5 * matmul(s2, out2)
-    result = layer_norm(x4, gain[5], shift[5]).astype(BF16)
+    ob = made["attended_out"]
+    o = ob.astype(F32).reshape(length, heads, head_dim)
+    z = jnp.concatenate([made["gates_out"][0], made["gates_out"][1]], axis=1).astype(F32)
+    padded = made["gated_out"][8 - half_taps : length + 8 + half_taps]
     _, back = jax.vjp(layer_norm, x4, gain[5], shift[5])
     dx4, gain5, shift5 = back(cot)
     df2 = (0.5 * dx4).astype(BF16)

time: 872 us -> 813 us (0.932)
  matrix products: 159 us -> 117 us
  Pallas kernels: 616 us -> 601 us
    pallas_call x2 -> x1, Pallas kernels: 115 us -> 59 us  [exchange(): pl.pallas_call(functools.partial(exchange_kernel, count, to_utterances),...]
    pallas_call x1, Pallas kernels: 220 us -> 261 us  [forward(): pl.pallas_call(body, out_shape=list(outs.values()) + [jax.ShapeDtypeStruc...]
    dot_general x10 -> x0, matrix products: 39.1 us -> none  [the longest x8 35.8 us: matmul(): return jnp.dot(left_side, right_side, preferred_element_type=jnp.float32)]
    dot_general x8, matrix products: 54.2 us -> 44.9 us  [matmul_left_t(): lax.dot_general(left_side, right_side, (((0,), (0,)), ((), ())), preferre...]
where the time goes in v2:
time: 813 us; the launch traced here: 802 us
  Pallas kernels  601 us (74%)
  matrix products  117 us (14%)
  other arithmetic  53.3 us (7%)
  local copies, waits for them, and re-layouts  29.1 us (4%)
    pallas_call x1, Pallas kernels, scatter(): pl.pallas_call(functools.partial(scatter_kernel, units, count), out_shape...  281 us
    pallas_call x1, Pallas kernels, forward(): pl.pallas_call(body, out_shape=list(outs.values()) + [jax.ShapeDtypeStruc...  261 us
    pallas_call x1, Pallas kernels, exchange(): pl.pallas_call(functools.partial(exchange_kernel, count, to_utterances),...  59 us
    dot_general x8, matrix products, matmul_right_t(): lax.dot_general(left_side, right_side, (((1,), (1,)), ((), ())), preferre...  49.6 us
    dot_general x8, matrix products, matmul_left_t(): lax.dot_general(left_side, right_side, (((0,), (0,)), ((), ())), preferre...  44.9 us

profile of v2, /device:TPU:1, one launch (start us, length us, event | category | flops | bytes accessed | tf_op | source)
XLA Modules:
  0.0 802.2 jit_solution(7555747246808512182)
XLA Ops:
  2.8 2.7 broadcast_select_fusion.refs_0_
  6.8 260.8 %shard_map.255 = (bf16[8,64,1024]{2,1,0:T(8,128)(2,1)}, bf16[8,64,1024]{2,1,0:T(8,128)(2,1)}, bf16[512,4096]{1,0:T(8,128)(2,1)}, f32[512,1024]{1,0:T(8,128)}, bf...) custom-call(bf16[8,64,1024]{2,1,0:T(8,128)(2,1)} %broadcast_select_f, ...), custom_call_target="tpu_custom_call" | custom-call | tf_op jit(solution)/shard_map/pallas_call | solution.py:1267
  274.6 2.7 fusion.30
  278.1 12.5 %fusion.6 = bf16[512,4096]{1,0:T(8,128)(2,1)S(1)} fusion(bf16[512,4096]{1,0:T(8,128)(2,1)} %get-tuple-element.51, bf16[4096,1024]{1,0:T(8,128)(2,1)} %bitcast.167, f32[512,1024]{1,0:T(8,128)S(1)} %get-tuple-element.114, f32[512]{0:T(512)S(1)} %negate_multiply_fusion.5), kind=kOutput, calls=%fused_computation.14 | convolution fusion | flops 4319608832 | bytes 18876416 | tf_op jit(solution)/shard_map/dot_general | solution.py:56
  290.7 5.0 multiply_reduce_fusion.1
  311.4 2.8 fusion.33
  314.2 2.8 multiply_reduce_fusion.3
  324.3 3.6 slice_bitcast_fusion
  332.5 8.7 %fusion.113 = (f32[8,512]{1,0:T(8,128)S(1)}, f32[8,512,512]{1,2,0:T(8,128)}) fusion(f32[512,512]{0,1:T(8,128)} %abs_multiply_fusion, f32[8]{0:T(128)S(1)} %copy-done.53, pred[512]{0:T(512)(128)(4,1)S(1)} %get-tuple-element.153, bf16[512,8,128]{0,2,1:T(8,128)(2,1)} %bitcast.125, bf16[512,8,128]{0,2,1:T(8,128)(2,1)} %bitcast.127), kind=kOutput, calls=%fused_computation.221 | convolution fusion | flops 549454336 | bytes 11551264 | tf_op jit(solution)/shard_map/sub | solution.py:1341
  341.2 6.3 fusion.54
  350.7 5.0 multiply_reduce_fusion
  360.9 4.1 multiply_reduce_fusion.4
  368.5 10.5 %fusion.13 = bf16[512,4096]{1,0:T(8,128)(2,1)S(1)} fusion(bf16[512,4096]{1,0:T(8,128)(2,1)} %get-tuple-element.66, bf16[4096,1024]{1,0:T(8,128)(2,1)} %bitcast.163, f32[512,1024]{1,0:T(8,128)} %add_add_fusion.6), kind=kOutput, calls=%fused_computation.21 | convolution fusion | flops 4319084544 | bytes 18874368 | tf_op jit(solution)/shard_map/dot_general | solution.py:56
  379.1 11.1 %fusion.105 = (bf16[1024]{0:T(1024)(128)(2,1)S(1)}, f32[512]{0:T(512)S(1)}, f32[512,1024]{1,0:T(8,128)}) fusion(f32[1024]{0:T(1024)S(1)} %bitcast.136, f32[512]{0:T(512)S(1)} %div.190, bf16[8,64,1024]{2,1,0:T(8,128)(2,1)S(1)} %copy-done.9, bf16[512,4096]{1,0:T(8,128)(2,1)S(1)} %fusion.13, bf16[1024,4096]{1,0:T(8,128)(2,1)} %bitcast.162), kind=kOutput, calls=%fused_computation.213 | convolution fusion | flops 4298111488 | bytes 15738880 | tf_op jit(solution)/shard_map/dot_general | solution.py:56
  390.7 3.8 multiply_reduce_fusion.5
  399.0 59.0 %shard_map.256 = (bf16[8,64,1024]{2,1,0:T(8,128)(2,1)}, bf16[8,64,1024]{2,1,0:T(8,128)(2,1)}, bf16[8,32,1024]{2,1,0:T(8,128)(2,1)}) custom-call(bf16[8,64,1024]{2,1,0:T(8,128)(2,1)} %bitcast.131, bf16[8,64,1024]{2,1,0:T(8,128)(2,1)} %bitcast.124, bf16[8,32,1024]{2,1,0:T(8,128)(2,1)} %broadcast_in_dim.76.refs_2_), custom_call_target="tpu_custom_call" | custom-call | tf_op jit(solution)/shard_map/pallas_call | solution.py:510
  458.0 2.8 convert_select_fusion
  460.9 9.3 %convolution_convert_fusion.3 = bf16[1024,4096]{1,0:T(8,128)(2,1)} fusion(bf16[512,1024]{1,0:T(8,128)(2,1)S(1)} %copy-done.35, bf16[512,4096]{1,0:T(8,128)(2,1)} %copy-done.60), kind=kOutput, calls=%fused_computation.30 | convolution fusion | flops 4299161600 | bytes 13631488 | tf_op jit(solution)/shard_map/dot_general | solution.py:62
  470.2 7.1 convolution_convert_fusion.2
  477.3 6.0 convolution_convert_fusion.4
  486.2 2.7 convolution_convert_fusion.5
  490.6 9.6 %convolution_convert_fusion.1 = bf16[1024,4096]{1,0:T(8,128)(2,1)} fusion(bf16[512,4096]{1,0:T(8,128)(2,1)} %copy-done.61, f32[512,1024]{1,0:T(8,128)S(1)} %copy-done.3, f32[1024]{0:T(1024)S(1)} %bitcast.157, f32[512]{0:T(512)S(1)} %copy-done.47, f32[512]{0:T(512)S(1)} %copy-done.41, f32[1024]{0:T(1024)S(1)} %bitcast.146), kind=kOutput, calls=%fused_computation.28 | convolution fusion | flops 4301783040 | bytes 14692352 | tf_op jit(solution)/shard_map/dot_general | solution.py:62
  500.2 7.4 convolution_convert_fusion
  507.6 281.1 %shard_map.257 = (bf16[128,4096]{1,0:T(8,128)(2,1)S(1)}, bf16[512,1024]{1,0:T(8,128)(2,1)S(1)}, bf16[128,3072]{1,0:T(8,128)(2,1)S(1)}, bf16[128,1024]{1,0:T(8,12...) custom-call(bf16[4,2,128,4096]{3,2,1,0:T(8,128)(2,1)} %bitcast.119, ...), custom_call_target="tpu_custom_call" | custom-call | tf_op jit(solution)/shard_map/pallas_call | solution.py:781
  (248 shorter events, 72.8 us)
Async XLA Ops:
  0.7 5.5 copy-start.53
  269.6 26.0 %copy-start.40 = (f32[512]{0:T(512)}, f32[512]{0:T(512)S(1)}, u32[]{:S(2)}) copy-start(f32[512]{0:T(512)S(1)} %broadcast_multiply_fusion.4) | copy-start | bytes 6148
  271.6 24.1 %copy-start.46 = (f32[512]{0:T(512)}, f32[512]{0:T(512)S(1)}, u32[]{:S(2)}) copy-start(f32[512]{0:T(512)S(1)} %fusion.89) | copy-start | bytes 6148
  272.2 23.4 %copy-start.42 = (f32[1,1,1024]{2,1,0:T(1,128)}, f32[1,1,1024]{2,1,0:T(1,128)S(1)}, u32[]{:S(2)}) copy-start(f32[1,1,1024]{2,1,0:T(1,128)S(1)} %get-tuple-element.131) | copy-start | bytes 12292
  277.3 13.3 %slice-start = ((s8[8388608]{0:T(1024)(128)(4,1)}), s8[4194304]{0:T(1024)(128)(4,1)S(1)}, s32[]{:S(2)}) async-start(s8[8388608]{0:T(1024)(128)(4,1)} %bitcast.164), calls=%async_computation | async-start | bytes 8388608
  278.1 18.3 %copy-start.17 = (f32[512,1024]{1,0:T(8,128)}, f32[512,1024]{1,0:T(8,128)S(1)}, u32[]{:S(2)}) copy-start(f32[512,1024]{1,0:T(8,128)S(1)} %get-tuple-element.114) | copy-start | bytes 6291460
  278.1 18.3 %copy-start.48 = (f32[512]{0:T(512)}, f32[512]{0:T(512)S(1)}, u32[]{:S(2)}) copy-start(f32[512]{0:T(512)S(1)} %negate_multiply_fusion.5) | copy-start | bytes 6148
  278.1 12.5 %copy-start.2 = (f32[512,1024]{1,0:T(8,128)S(1)}, f32[512,1024]{1,0:T(8,128)}, u32[]{:S(2)}) copy-start(f32[512,1024]{1,0:T(8,128)} %get-tuple-element.53) | copy-start | bytes 6291460
  278.1 12.5 %slice-start.1 = ((s8[8388608]{0:T(1024)(128)(4,1)}), s8[4194304]{0:T(1024)(128)(4,1)S(1)}, s32[]{:S(2)}) async-start(s8[8388608]{0:T(1024)(128)(4,1)} %bitcast.164), calls=%async_computation.1 | async-start | bytes 8388608
  341.2 6.3 copy-start.30
  350.7 5.0 copy-start.21
  358.8 6.2 copy-start.23
  379.1 11.1 %copy-start.60 = (bf16[512,4096]{1,0:T(8,128)(2,1)}, bf16[512,4096]{1,0:T(8,128)(2,1)S(1)}, u32[]{:S(2)}) copy-start(bf16[512,4096]{1,0:T(8,128)(2,1)S(1)} %fusion.13) | copy-start | bytes 12582916
  396.3 61.7 %copy-start.45 = (pred[8,64]{1,0:T(8,128)(4,1)S(1)}, pred[8,64]{1,0:T(8,128)(4,1)}, u32[]{:S(2)}) copy-start(pred[8,64]{1,0:T(8,128)(4,1)} %copy-done.44) | copy-start | bytes 1540
  460.9 9.3 %copy-start.15 = (f32[512,1024]{1,0:T(8,128)S(1)}, f32[512,1024]{1,0:T(8,128)}, u32[]{:S(2)}) copy-start(f32[512,1024]{1,0:T(8,128)} %add_add_fusion.6) | copy-start | bytes 6291460
  460.9 9.3 %copy-start.55 = (bf16[512,4096]{1,0:T(8,128)(2,1)S(1)}, bf16[512,4096]{1,0:T(8,128)(2,1)}, u32[]{:S(2)}) copy-start(bf16[512,4096]{1,0:T(8,128)(2,1)} %get-tuple-element.66) | copy-start | bytes 12582916
  470.2 7.1 copy-start.8
  470.2 7.1 copy-start.24
  470.2 7.1 copy-start.52
  477.3 6.0 copy-start.13
  477.3 6.0 copy-start.31
  490.6 9.6 %copy-start.18 = (f32[512,1024]{1,0:T(8,128)S(1)}, f32[512,1024]{1,0:T(8,128)}, u32[]{:S(2)}) copy-start(f32[512,1024]{1,0:T(8,128)} %copy-done.17) | copy-start | bytes 6291460
  490.6 9.6 %copy-start.49 = (f32[512]{0:T(512)S(1)}, f32[512]{0:T(512)}, u32[]{:S(2)}) copy-start(f32[512]{0:T(512)} %copy-done.48) | copy-start | bytes 6148
  490.6 9.6 %copy-start.54 = (bf16[512,4096]{1,0:T(8,128)(2,1)S(1)}, bf16[512,4096]{1,0:T(8,128)(2,1)}, u32[]{:S(2)}) copy-start(bf16[512,4096]{1,0:T(8,128)(2,1)} %get-tuple-element.51) | copy-start | bytes 12582916
  (42 other events, 105.7 us)

commit v3 on v0

--- a/solution.py
+++ b/solution.py
@@ -1,7 +1,17 @@
+import functools
+import types
+
 import jax
 import jax.numpy as jnp
 from jax import lax
+from jax.experimental import pallas as pl
+from jax.experimental.pallas import tpu as pltpu
 from jax.sharding import PartitionSpec as P
+
+MESH = pl.DeviceIdType.MESH
+BF16 = jnp.bfloat16
+F32 = jnp.float32
+ANY = pl.BlockSpec(memory_space=pl.ANY)
 
 SPAN = 10
 
@@ -65,7 +75,7 @@
     return (jnp.where(key_live[:, None, None, :], scores, NEGATIVE), distance)
 
 
-def per_device(
+def per_device_any(
     frames_in,
     noise,
     lengths,
@@ -376,6 +386,1245 @@
     )
 
 
+def place():
+    seq, dp = lax.axis_index("seq"), lax.axis_index("dp")
+    return seq // 2, lax.rem(seq, 2), dp // 2, lax.rem(dp, 2)
+
+
+def device(z, x, y, core):
+    return (z * 2 + x, y * 2 + core)
+
+
+def z_partners(z):
+    return (z + 1 - 2 * lax.rem(z, 2), lax.rem(z + 2, 4), 3 - z)
+
+
+def remote(source, target, send, recv, where):
+    return pltpu.make_async_remote_copy(
+        src_ref=source,
+        dst_ref=target,
+        send_sem=send,
+        recv_sem=recv,
+        device_id=where,
+        device_id_type=MESH,
+    )
+
+
+def greet(partners, waits):
+    barrier = pltpu.get_barrier_semaphore()
+    for partner in partners:
+        pl.semaphore_signal(barrier, inc=1, device_id=partner, device_id_type=MESH)
+    pl.semaphore_wait(barrier, waits)
+
+
+def utterance_of(z, x, core):
+    return lax.rem(z, 2) * 4 + x * 2 + core
+
+
+def home_of(utterance, y, group):
+    return device(2 * group + utterance // 4, lax.rem(utterance // 2, 2), y, lax.rem(utterance, 2))
+
+
+def bits_of(s):
+    return s // 4, lax.rem(s // 2, 2), lax.rem(s, 2)
+
+
+def flipped(bits, r):
+    flips = (r // 4, r // 2 % 2, r % 2)
+    return [1 - b if f else b for b, f in zip(bits, flips)]
+
+
+def utterance_in_round(seq, r):
+    b2, b1, b0 = bits_of(seq)
+    out = flipped((b1, b0, b2), r)
+    return out[0] * 4 + out[1] * 2 + out[2]
+
+
+def seq_in_round(utterance, r):
+    t2, t1, t0 = flipped(bits_of(utterance), r)
+    return t0 * 4 + t2 * 2 + t1
+
+
+def units_of(shapes):
+    units = []
+    for index, (rows, columns) in enumerate(shapes):
+        for row in range(0, rows, 128):
+            for column in range(0, columns, 1024):
+                units.append((index, row, column))
+    return units
+
+
+ROWS = 128
+HALF = 64
+COLUMNS = 1024
+LAGS = (0, 1, 2, 3, 5, 7, 8)
+SPLIT = 384
+
+
+def blocks(rows, size):
+    def run(body):
+        @pl.loop(0, rows // size, unroll=2)
+        def _(i):
+            body(pl.ds(pl.multiple_of(i * size, size), size))
+
+    return run
+
+
+def normalise(v, norm, i):
+    average = jnp.mean(v, axis=-1, keepdims=True)
+    centred = v - average
+    variance = jnp.mean(centred * centred, axis=-1, keepdims=True)
+    return centred * lax.rsqrt(variance + EPSILON) * norm[i, 0:1, :] + norm[i, 1:2, :]
+
+
+TILE = 256
+
+
+def sigmoid(v):
+    return 0.5 * jnp.tanh(0.5 * v) + 0.5
+
+
+def silu(v):
+    return v * sigmoid(v)
+
+
+def times_unit(left, weight, emit, poll):
+    unit, loads = weight
+    for n in range(COLUMNS // TILE):
+        columns = pl.ds(n * TILE, TILE)
+        loads[n].wait()
+        emit(columns, jnp.dot(left[...], unit[:, :, :, columns].reshape(COLUMNS, TILE), preferred_element_type=F32))
+        poll()
+
+
+def score_block(q, k, slope_row, first, live_keys):
+    shape = (q.shape[0], k.shape[0])
+    scores = lax.dot_general(q, k, (((1,), (1,)), ((), ())), preferred_element_type=F32)
+    rows = lax.broadcasted_iota(jnp.int32, shape, 0) + first
+    keys = lax.broadcasted_iota(jnp.int32, shape, 1)
+    distance = jnp.abs(rows - keys).astype(F32) * (1.0 / k.shape[0])
+    scores = scores * (q.shape[1] ** -0.5) - slope_row * distance
+    return jnp.where(keys.astype(F32) < live_keys, scores, NEGATIVE), distance
+
+
+def softmax_block(scores):
+    top = jnp.max(scores, axis=-1, keepdims=True)
+    expd = jnp.exp(scores - top)
+    return expd / jnp.sum(expd, axis=-1, keepdims=True)
+
+
+QUERIES = 128
+BLOCK = 32
+
+
+def forward_kernel(units, names, *refs):
+    r = types.SimpleNamespace(**dict(zip(names, refs)))
+    norm, taps, slope = r.norm, r.taps, r.slope
+    length, width = r.x.shape[1:]
+    heads = slope.shape[0]
+    head_dim = width // heads
+    z, x, y, core = place()
+    seq, group = z * 2 + x, z // 2
+    utterance = utterance_of(z, x, core)
+    same = group == core
+    zs = z_partners(z)
+    over_z = [device(other, x, y, core) for other in zs]
+    over_x = device(z, 1 - x, y, core)
+    over_y = device(z, x, 1 - y, core)
+    over_core = device(z, x, y, 1 - core)
+    mates = [utterance_in_round(seq, i) for i in range(8)]
+    givers = [device(s // 2, lax.rem(s, 2), y, group) for s in [seq_in_round(utterance, i) for i in range(8)]]
+    targets = [home_of(u, y, core) for u in mates]
+    barrier = pltpu.get_barrier_semaphore()
+
+    @pl.when(jnp.logical_not(same))
+    def _():
+        pl.semaphore_signal(barrier, inc=1, device_id=givers[0], device_id_type=MESH)
+
+    for partner in givers[1:] + [over_z[0], over_z[2], over_x, over_y, over_core]:
+        pl.semaphore_signal(barrier, inc=1, device_id=partner, device_id_type=MESH)
+    pl.semaphore_wait(barrier, jnp.where(same, 12, 13))
+
+    swaps = ((r.start, r.h0), (r.lens, r.lens_here), (r.cot, r.cot_out))
+
+    def swap(i, j):
+        source, target = swaps[i]
+        return remote(source.at[mates[j]], target.at[seq], r.swap_send.at[i, j], r.swap_recv.at[i, j], targets[j])
+
+    def swap_local(i):
+        source, target = swaps[i]
+        return pltpu.make_async_copy(source.at[mates[0]], target.at[seq], r.swap_own.at[i])
+
+    def swap_start(i, j):
+        if j > 0:
+            swap(i, j).start()
+            return
+
+        @pl.when(jnp.logical_not(same))
+        def _():
+            swap(i, 0).start()
+
+        @pl.when(same)
+        def _():
+            swap_local(i).start()
+
+    def swap_wait(i):
+        @pl.when(jnp.logical_not(same))
+        def _():
+            swap(i, 0).wait()
+
+        @pl.when(same)
+        def _():
+            swap_local(i).wait()
+
+        for j in range(1, 8):
+            swap(i, j).wait()
+
+    send, recv, own = r.send, r.recv, r.own
+    shards, fulls = r.shards, r.fulls
+
+    def spot(unit):
+        index, row, column = unit
+        rows = pl.ds(row + pl.multiple_of(core * HALF, HALF), HALF)
+        mine = pl.ds(column + pl.multiple_of(y * SPLIT, 128), COLUMNS - SPLIT)
+        third = pl.ds(column + pl.multiple_of(y * (COLUMNS - SPLIT), 128), SPLIT)
+        return shards[index], fulls[index], rows, mine, third, pl.ds(column, COLUMNS)
+
+    middle = (z == 1) | (z == 2)
+    near_pair, far_pair = pl.ds(2 * (z // 2), 2), pl.ds(2 - 2 * (z // 2), 2)
+
+    class Along:
+        def __init__(self, copy, sends, gets):
+            self.copy, self.sends, self.gets = copy, sends, gets
+
+        def start(self):
+            @pl.when(self.sends)
+            def _():
+                self.copy.start()
+
+        def wait(self):
+            @pl.when(self.sends)
+            def _():
+                self.copy.wait_send()
+
+            @pl.when(self.gets)
+            def _():
+                self.copy.wait_recv()
+
+    def first(u):
+        shard, full, rows, mine, _, _ = spot(units[u])
+        every = pl.ds(units[u][2], COLUMNS)
+        return [
+            remote(shard.at[rows, mine], full.at[z, x, rows, mine], send.at[u, 0], recv.at[u, 0], over_z[0]),
+            pltpu.make_async_copy(shard.at[rows, every], full.at[z, x, rows, every], own.at[u]),
+        ]
+
+    def across(u):
+        _, full, rows, mine, _, _ = spot(units[u])
+        piece = full.at[near_pair, x, rows, mine]
+        return [Along(remote(piece, piece, send.at[u, 1], recv.at[u, 1], over_z[2]), middle, middle)]
+
+    def outward(u):
+        _, full, rows, mine, _, _ = spot(units[u])
+        piece = full.at[far_pair, x, rows, mine]
+        copy = remote(piece, piece, send.at[u, 2], recv.at[u, 2], over_z[0])
+        return [Along(copy, middle, jnp.logical_not(middle))]
+
+    def second(u):
+        _, full, rows, mine, _, _ = spot(units[u])
+        piece = full.at[:, x, rows, mine]
+        return [remote(piece, piece, send.at[u, 3], recv.at[u, 3], over_x)]
+
+    def third(u):
+        _, full, rows, _, part, _ = spot(units[u])
+        pieces = [full.at[:, 1 - x, rows, part]] + [full.at[other, x, rows, part] for other in zs]
+        out = [remote(p, p, send.at[u, 4 + j], recv.at[u, 4 + j], over_y) for j, p in enumerate(pieces)]
+        return out
+
+    def fourth(u):
+        _, full, rows, _, _, whole = spot(units[u])
+        piece = full.at[:, :, rows, whole]
+        return [remote(piece, piece, send.at[u, 8], recv.at[u, 8], over_core)]
+
+    stages = (first, across, outward, second, third, fourth)
+    last = len(units)
+    done = [0]
+
+    actions = []
+    ends = {}
+
+    def move(u, depth):
+        def act_on():
+            if depth > 0:
+                for copy in stages[depth - 1](u):
+                    copy.wait()
+            if depth < len(stages):
+                for copy in stages[depth](u):
+                    copy.start()
+
+        return act_on
+
+    for step in range(last + LAGS[-1]):
+        for depth, lag in enumerate(LAGS):
+            if 0 <= step - lag < last:
+                actions.append(move(step - lag, depth))
+                if depth == len(stages):
+                    ends[step - lag] = len(actions)
+        if 12 <= step < 20:
+            actions.append(functools.partial(swap_start, 2, step - 12))
+
+    def poll(count=1):
+        for _ in range(count):
+            if done[0] < len(actions):
+                actions[done[0]]()
+                done[0] += 1
+
+    taken = [0]
+
+    def weight():
+        u = taken[0]
+        taken[0] += 1
+        while done[0] < ends[u]:
+            poll()
+        index, row, column = units[u]
+        loads = []
+        for n in range(COLUMNS // TILE):
+            source = fulls[index].at[:, :, pl.ds(row, ROWS), pl.ds(column + n * TILE, TILE)]
+            target = r.unit.at[u % 2, :, :, :, pl.ds(n * TILE, TILE)]
+            copy = pltpu.make_async_copy(source, target, r.load.at[u % 2, n])
+            copy.start()
+            loads.append(copy)
+        return r.unit.at[u % 2], loads
+
+    kept = []
+
+    def keep(source, target):
+        copy = pltpu.make_async_copy(source, target, r.kept.at[len(kept)])
+        copy.start()
+        kept.append(copy)
+
+    xs, act, acc = r.x, r.act, r.acc
+    poll()
+    for j in range(8):
+        swap_start(0, j)
+    for j in range(8):
+        swap_start(1, j)
+    poll(4)
+    swap_wait(0)
+
+    @blocks(length, BLOCK)
+    def _(rows):
+        xs[0, rows, :] = r.h0[rows.start // 64, pl.ds(pl.multiple_of(lax.rem(rows.start, 64), BLOCK), BLOCK), :].astype(F32)
+        act[rows, :] = normalise(xs[0, rows, :], norm, 0).astype(BF16)
+
+    keep(r.h0, r.h0_out)
+
+    def feed_forward(x_in, x_out, up, up_out):
+        hidden = r.hidden
+        for p in range(4):
+            unit, loads = weight()
+
+            for n in range(COLUMNS // TILE):
+                columns = pl.ds(n * TILE, TILE)
+                loads[n].wait()
+                value = jnp.dot(act[...], unit[:, :, :, columns].reshape(COLUMNS, TILE), preferred_element_type=F32)
+                up[p, :, columns] = value.astype(BF16)
+                value = silu(value).astype(BF16)
+                for t in range(2 * n, 2 * n + 2):
+                    place_at = pl.ds((2 * p + t // 4) * 128, 128)
+                    hidden[t % 4, :, place_at] = value[:, (t - 2 * n) * 128 : (t - 2 * n + 1) * 128]
+                poll()
+
+            keep(up.at[p], up_out.at[:, pl.ds(p * COLUMNS, COLUMNS)])
+        for q in range(4):
+            def emit(columns, value, q=q):
+                if q == 0:
+                    acc[:, columns] = value
+                else:
+                    acc[:, columns] = acc[:, columns] + value
+
+            times_unit(hidden.at[q], weight(), emit, poll)
+
+        @blocks(length, BLOCK)
+        def _(rows):
+            xs[x_out, rows, :] = xs[x_in, rows, :] + 0.5 * acc[rows, :]
+
+    feed_forward(0, 1, r.up, r.u1_out)
+    keep(xs.at[1], r.x1_out)
+
+    @blocks(length, BLOCK)
+    def _(rows):
+        act[rows, :] = normalise(xs[1, rows, :], norm, 1).astype(BF16)
+
+    qkv = r.qkv
+    for i in range(3):
+
+        def emit(columns, value, i=i):
+            qkv[i, :, columns] = value.astype(BF16)
+
+        times_unit(act, weight(), emit, poll)
+    keep(qkv, r.qkv_out)
+    swap_wait(1)
+    live_count = r.lens_here[0, 0:1, 0:1]
+    keep(r.lens_here, r.lens_out)
+    attended = r.attended
+    for h in range(heads):
+        columns = pl.ds(h * head_dim, head_dim)
+
+        @blocks(length, QUERIES)
+        def _(rows, h=h, columns=columns):
+            scores, _ = score_block(
+                qkv[0, rows, columns], qkv[1, :, columns], slope[h : h + 1, :], rows.start, live_count
+            )
+            prob = softmax_block(scores).astype(BF16)
+            attended[rows, columns] = jnp.dot(prob, qkv[2, :, columns], preferred_element_type=F32).astype(BF16)
+
+        poll(2)
+    keep(attended, r.attended_out)
+
+    def add_to(x_in, x_out):
+        def emit(columns, value):
+            xs[x_out, :, columns] = xs[x_in, :, columns] + value
+
+        return emit
+
+    times_unit(attended, weight(), add_to(1, 2), poll)
+    keep(xs.at[2], r.x2_out)
+
+    @blocks(length, BLOCK)
+    def _(rows):
+        act[rows, :] = normalise(xs[2, rows, :], norm, 2).astype(BF16)
+
+    gates, gated = r.gates, r.gated
+
+    def emit(columns, value):
+        acc[:, columns] = value
+        gates[0, :, columns] = value.astype(BF16)
+
+    times_unit(act, weight(), emit, poll)
+    gated[0:8, :] = jnp.zeros((8, width), F32)
+    gated[length + 8 : length + 16, :] = jnp.zeros((8, width), F32)
+
+    def emit(columns, value):
+        gates[1, :, columns] = value.astype(BF16)
+        live = lax.broadcasted_iota(jnp.int32, value.shape, 0).astype(F32) < live_count
+        passed = jnp.where(live, acc[:, columns] * sigmoid(value), 0.0)
+        gated[pl.ds(8, length), columns] = passed.astype(BF16).astype(F32)
+
+    times_unit(act, weight(), emit, poll)
+    keep(gates, r.gates_out)
+    keep(gated, r.gated_out)
+    depth = r.depth
+
+    @blocks(length, BLOCK)
+    def _(rows):
+        near = gated[pl.ds(pl.multiple_of(rows.start, BLOCK), BLOCK + 16), :]
+        total = taps[0:1, :] * near[6 : 6 + BLOCK]
+        for t in range(1, taps.shape[0]):
+            total = total + taps[t : t + 1, :] * near[6 + t : 6 + t + BLOCK]
+        depth[rows, :] = total
+        value = normalise(total, norm, 3)
+        act[rows, :] = (silu(value)).astype(BF16)
+
+    keep(depth, r.depth_out)
+    times_unit(act, weight(), add_to(2, 3), poll)
+    keep(xs.at[3], r.x3_out)
+
+    @blocks(length, BLOCK)
+    def _(rows):
+        act[rows, :] = normalise(xs[3, rows, :], norm, 4).astype(BF16)
+
+    feed_forward(3, 4, r.up2, r.u2_out)
+    keep(xs.at[4], r.x4_out)
+
+    @blocks(length, BLOCK)
+    def _(rows):
+        act[rows, :] = normalise(xs[4, rows, :], norm, 5).astype(BF16)
+
+    keep(act, r.result_out)
+    swap_wait(2)
+    for copy in kept:
+        copy.wait()
+
+
+def forward(start, lens, cot, norm, taps, slope, shards, collective_id):
+    shapes = [s.shape for s in shards]
+    units = units_of(shapes)
+    width = norm.shape[-1]
+    frames = start.shape[1]
+    length = 8 * frames
+    count = len(shards)
+    dma = pltpu.SemaphoreType.DMA
+    hidden = shapes[0][1]
+    wide = lambda *lead: jax.ShapeDtypeStruct(lead + (length, width), F32)
+    low = lambda *lead: jax.ShapeDtypeStruct(lead + (length, width), BF16)
+    up = jax.ShapeDtypeStruct((length, hidden), BF16)
+    outs = dict(
+        cot_out=jax.ShapeDtypeStruct(cot.shape, cot.dtype),
+        h0_out=jax.ShapeDtypeStruct(start.shape, start.dtype),
+        u1_out=up,
+        x1_out=wide(),
+        qkv_out=low(3),
+        attended_out=low(),
+        x2_out=wide(),
+        gates_out=low(2),
+        gated_out=jax.ShapeDtypeStruct((length + 16, width), F32),
+        depth_out=wide(),
+        x3_out=wide(),
+        u2_out=up,
+        x4_out=wide(),
+        result_out=low(),
+        lens_out=jax.ShapeDtypeStruct(lens.shape, lens.dtype),
+    )
+    scratch = dict(
+        h0=pltpu.VMEM(start.shape, BF16),
+        lens_here=pltpu.VMEM(lens.shape, F32),
+        x=pltpu.VMEM((5, length, width), F32),
+        act=pltpu.VMEM((length, width), BF16),
+        acc=pltpu.VMEM((length, width), F32),
+        hidden=pltpu.VMEM((4, length, width), BF16),
+        up=pltpu.VMEM((4, length, width), BF16),
+        up2=pltpu.VMEM((4, length, width), BF16),
+        qkv=pltpu.VMEM((3, length, width), BF16),
+        attended=pltpu.VMEM((length, width), BF16),
+        gates=pltpu.VMEM((2, length, width), BF16),
+        gated=pltpu.VMEM((length + 16, width), F32),
+        depth=pltpu.VMEM((length, width), F32),
+        unit=pltpu.VMEM((2, 4, 2, ROWS, COLUMNS), BF16),
+        load=dma((2, COLUMNS // TILE)),
+        swap_send=dma((3, 8)),
+        swap_recv=dma((3, 8)),
+        swap_own=dma((3,)),
+        send=dma((len(units), 9)),
+        recv=dma((len(units), 9)),
+        own=dma((len(units),)),
+        kept=dma((32,)),
+    )
+    names = ["start", "lens", "cot", "norm", "taps", "slope"]
+    vmem = pl.BlockSpec(memory_space=pltpu.VMEM)
+
+    def body(*refs):
+        plain, rest = refs[:6], refs[6:]
+        ours, rest = rest[:count], rest[count:]
+        made, rest = rest[: len(outs)], rest[len(outs) :]
+        fulls, rest = rest[:count], rest[count:]
+        forward_kernel(
+            units,
+            names + list(outs) + list(scratch) + ["shards", "fulls"],
+            *plain,
+            *made,
+            *rest,
+            ours,
+            fulls,
+        )
+
+    results = pl.pallas_call(
+        body,
+        out_shape=list(outs.values()) + [jax.ShapeDtypeStruct((4, 2) + s, BF16) for s in shapes],
+        in_specs=[ANY, ANY, ANY, vmem, vmem, vmem] + [ANY] * count,
+        out_specs=[ANY] * (len(outs) + count),
+        scratch_shapes=list(scratch.values()),
+        compiler_params=pltpu.CompilerParams(
+            collective_id=collective_id, has_side_effects=True, vmem_limit_bytes=60 * 2**20
+        ),
+    )(start, lens, cot, norm, taps, slope, *shards)
+    made = types.SimpleNamespace(**dict(zip(outs, results[: len(outs)])))
+    fulls = [f.reshape(8 * s[0], s[1]) for f, s in zip(results[len(outs) :], shapes)]
+    return made, fulls
+
+
+CADENCE = 12.0
+SLOTS = 5
+
+
+def norm_back(v, dy, norm, i, sums):
+    average = jnp.mean(v, axis=-1, keepdims=True)
+    centred = v - average
+    scale = lax.rsqrt(jnp.mean(centred * centred, axis=-1, keepdims=True) + EPSILON)
+    unit = centred * scale
+    sums[2 * i] += jnp.sum((dy * unit).reshape(-1, 8, dy.shape[-1]), axis=0)
+    sums[2 * i + 1] += jnp.sum(dy.reshape(-1, 8, dy.shape[-1]), axis=0)
+    inner = dy * norm[i, 0:1, :]
+    return scale * (
+        inner
+        - jnp.mean(inner, axis=-1, keepdims=True)
+        - unit * jnp.mean(inner * unit, axis=-1, keepdims=True)
+    )
+
+
+def silu_back(v):
+    s = sigmoid(v)
+    return s * (1.0 + v * (1.0 - s))
+
+
+def times_t(left, right):
+    return lax.dot_general(left, right, (((1,), (1,)), ((), ())), preferred_element_type=F32)
+
+
+def t_times(left, right):
+    return lax.dot_general(left, right, (((0,), (0,)), ((), ())), preferred_element_type=F32)
+
+
+BACK_ORDER = (7, 6, 5, 4, 3, 2, 1, 0)
+
+
+def backward_kernel(units, names, *refs):
+    r = types.SimpleNamespace(**dict(zip(names, refs)))
+    norm, taps, slope, sums = r.norm, r.taps, r.slope, r.sums
+    length, width = r.dx.shape
+    heads = slope.shape[0]
+    head_dim = width // heads
+    z, x, y, core = place()
+    seq, group = z * 2 + x, z // 2
+    utterance = utterance_of(z, x, core)
+    keeps = group == core
+    other = jnp.logical_not(keeps)
+    z_other = z + 1 - 2 * lax.rem(z, 2)
+    over_core = device(z, x, y, 1 - core)
+    over_x = device(z, 1 - x, y, core)
+    over_z = device(z_other, x, y, core)
+    far = device(3 - z, x, y, group)
+    seqs = [seq_in_round(utterance, i) for i in range(8)]
+    targets = [device(s // 2, lax.rem(s, 2), y, group) for s in seqs]
+    givers = [home_of(utterance_in_round(seq, i), y, core) for i in range(8)]
+    barrier = pltpu.get_barrier_semaphore()
+    for partner in [over_core, over_x, over_z] + givers[1:]:
+        pl.semaphore_signal(barrier, inc=1, device_id=partner, device_id_type=MESH)
+
+    @pl.when(other)
+    def _():
+        for giver in [device(3 - z, x, y, 0), device(3 - z, x, y, 1), givers[0]]:
+            pl.semaphore_signal(barrier, inc=1, device_id=giver, device_id_type=MESH)
+
+    pl.semaphore_wait(barrier, jnp.where(keeps, 11, 12))
+
+    swaps = ((r.result, r.result_home), (r.dframes, r.dframes_home), (r.small, r.small_home))
+
+    def swap(i, j):
+        source, target = swaps[i][0], swaps[i][1].at[utterance]
+        block = source if i == 2 else source.at[seqs[j]]
+        return remote(block, target, r.swap_send.at[i, j], r.swap_recv.at[i, j], targets[j])
+
+    def swap_local(i):
+        source, target = swaps[i][0], swaps[i][1].at[utterance]
+        return pltpu.make_async_copy(source if i == 2 else source.at[seqs[0]], target, r.swap_own.at[i])
+
+    def swap_start(i, j):
+        if j > 0:
+            swap(i, j).start()
+            return
+
+        @pl.when(other)
+        def _():
+            swap(i, 0).start()
+
+        @pl.when(keeps)
+        def _():
+            swap_local(i).start()
+
+    def swap_wait(i):
+        @pl.when(other)
+        def _():
+            swap(i, 0).wait()
+
+        @pl.when(keeps)
+        def _():
+            swap_local(i).wait()
+
+        for j in range(1, 8):
+            swap(i, j).wait()
+
+    grads, outs, mine, core_in, first_in, second_in = (
+        r.grads, r.outs, r.mine, r.core_in, r.first_in, r.second_in
+    )
+    half = pl.multiple_of(core * HALF, HALF)
+    other_half = pl.multiple_of((1 - core) * HALF, HALF)
+    last = len(units)
+
+    def columns_of(u):
+        return pl.ds(units[u][2], COLUMNS)
+
+    def core_copy(u):
+        source = grads[units[u][0]].at[:, :, pl.ds(units[u][1] + other_half, HALF), columns_of(u)]
+        return remote(source, core_in.at[u % 2], r.s_core.at[u % 2], r.r_core.at[u % 2], over_core)
+
+    def load_copy(u):
+        source = grads[units[u][0]].at[:, :, pl.ds(units[u][1] + half, HALF), columns_of(u)]
+        return pltpu.make_async_copy(source, mine.at[u % SLOTS], r.s_load.at[u % 2])
+
+    def swapped(u):
+        return u % 8 == 2
+
+    def first_copies(u):
+        slot = u % SLOTS
+        held, arriving, send, recv = mine.at[slot], first_in.at[slot], r.s_first.at[slot], r.r_first.at[slot]
+        if swapped(u):
+            return [
+                remote(held.at[t], arriving.at[pl.ds(2 * i, 2)], send.at[i], recv.at[i], over_z)
+                for i, t in enumerate((z_other, 3 - z_other))
+            ]
+        return [remote(held.at[:, 1 - x], arriving, send.at[0], recv.at[0], over_x)]
+
+    def second_copies(u):
+        slot = u % SLOTS
+        held, arriving, send, recv = mine.at[slot], second_in.at[slot], r.s_second.at[slot], r.r_second.at[slot]
+        if swapped(u):
+            pairs, partner = ((z, 1 - x), (3 - z, 1 - x)), over_x
+        else:
+            pairs, partner = ((z_other, x), (3 - z_other, x)), over_z
+        return [
+            remote(held.at[t, t_x], arriving.at[i], send.at[i], recv.at[i], partner)
+            for i, (t, t_x) in enumerate(pairs)
+        ]
+
+    def far_copy(u, giver=None):
+        start = half if giver is None else giver * HALF
+        target = outs[units[u][0]].at[pl.ds(units[u][1] + start, HALF), columns_of(u)]
+        recv = r.r_far.at[u, core if giver is None else giver]
+        return remote(mine.at[u % SLOTS, 3 - z, x], target, r.s_far.at[u % 2], recv, far)
+
+    def near_target(u, start):
+        return outs[units[u][0]].at[pl.ds(units[u][1] + start, HALF), columns_of(u)]
+
+    def near_copy(u, start):
+        return remote(
+            mine.at[u % SLOTS, z, x], near_target(u, start), r.s_near.at[u % 2], r.r_near.at[u], over_core
+        )
+
+    def near_local(u):
+        return pltpu.make_async_copy(mine.at[u % SLOTS, z, x], near_target(u, half), r.s_own.at[u % 2])
+
+    def add(into, more):
+        into[...] = (into[...].astype(F32) + more[...].astype(F32)).astype(BF16)
+
+    def stage0(u):
+        load_copy(u).start()
+        core_copy(u).start()
+
+    def stage1(u):
+        load_copy(u).wait()
+        core_copy(u).wait()
+        held, arrived = mine.at[u % SLOTS], core_in.at[u % 2]
+        if swapped(u):
+            sent = [(t, t_x) for t in (z_other, 3 - z_other) for t_x in (0, 1)]
+            rest = [(t, t_x) for t in (z, 3 - z) for t_x in (0, 1)]
+        else:
+            sent, rest = [(t, 1 - x) for t in range(4)], [(t, x) for t in range(4)]
+        for t in sent:
+            add(held.at[t], arrived.at[t])
+        for copy in first_copies(u):
+            copy.start()
+        for t in rest:
+            add(held.at[t], arrived.at[t])
+
+    def stage2(u):
+        for copy in first_copies(u):
+            copy.wait()
+        held, arrived = mine.at[u % SLOTS], first_in.at[u % SLOTS]
+        if swapped(u):
+            sent = [((t, 1 - x), 2 * i + 1 - x) for i, t in enumerate((z, 3 - z))]
+            rest = [((t, x), 2 * i + x) for i, t in enumerate((z, 3 - z))]
+        else:
+            sent = [((t, x), t) for t in (z_other, 3 - z_other)]
+            rest = [((t, x), t) for t in (z, 3 - z)]
+        for (t, i), copy in zip(sent, second_copies(u)):
+            add(held.at[t], arrived.at[i])
+            copy.start()
+        for t, i in rest:
+            add(held.at[t], arrived.at[i])
+
+    def stage3(u):
+        for copy in second_copies(u):
+            copy.wait()
+        held, arrived = mine.at[u % SLOTS], second_in.at[u % SLOTS]
+        add(held.at[3 - z, x], arrived.at[1])
+        far_copy(u).start()
+        add(held.at[z, x], arrived.at[0])
+
+        @pl.when(keeps)
+        def _():
+            near_local(u).start()
+
+        @pl.when(other)
+        def _():
+            near_copy(u, half).start()
+
+    def stage4(u):
+        far_copy(u).wait_send()
+
+        @pl.when(keeps)
+        def _():
+            near_local(u).wait()
+            near_copy(u, other_half).wait_recv()
+
+        @pl.when(other)
+        def _():
+            near_copy(u, half).wait_send()
+
+    order = ((stage1, 1), (stage0, 0), (stage2, 2), (stage3, 3), (stage4, 4))
+    ticks, emitted, clock = [0], [0], [0.0]
+
+    def tick():
+        step = ticks[0]
+        ticks[0] += 1
+        settle(min(step + 1, last))
+        for stage, depth in order:
+            if 0 <= step - depth < last:
+                stage(step - depth)
+
+    def spent(us):
+        if emitted[0] == 0:
+            return
+        clock[0] += us
+        while clock[0] >= CADENCE:
+            clock[0] -= CADENCE
+            if ticks[0] < emitted[0]:
+                tick()
+
+    stored = [0]
+
+    def stage_copy(u):
+        target = grads[units[u][0]].at[:, :, pl.ds(units[u][1], ROWS), columns_of(u)]
+        return pltpu.make_async_copy(r.stage.at[u % 2], target, r.s_stage.at[u % 2])
+
+    def settle(count):
+        while stored[0] < count:
+            stage_copy(stored[0]).wait()
+            stored[0] += 1
+
+    def emit(left, right):
+        u = emitted[0]
+        stage = r.stage.at[u % 2]
+        settle(u - 1)
+        for t in range(4):
+            value = t_times(left[:, pl.ds(t * 256, 256)], right[...])
+            stage[t] = value.astype(BF16).reshape(2, ROWS, COLUMNS)
+        stage_copy(u).start()
+        emitted[0] += 1
+        if u == 0:
+            tick()
+        spent(3.0)
+
+    wanted = []
+    for index in BACK_ORDER:
+        rows, columns = r.fulls[index].shape
+        for row in range(0, rows, 1024):
+            for column in range(0, columns, 1024):
+                wanted.append((index, row, column))
+
+    def weight_copies(i):
+        index, row, column = wanted[i]
+        return [
+            pltpu.make_async_copy(
+                r.fulls[index].at[pl.ds(row + 256 * t, 256), pl.ds(column, 1024)],
+                r.unit.at[i % 2, t],
+                r.s_unit.at[i % 2, t],
+            )
+            for t in range(4)
+        ]
+
+    taken = [0]
+
+    def weight():
+        i = taken[0]
+        taken[0] += 1
+        if i + 1 < len(wanted):
+            for copy in weight_copies(i + 1):
+                copy.start()
+        return r.unit.at[i % 2], weight_copies(i)
+
+    def times_matrix(left, take):
+        unit, copies = weight()
+        for t in range(4):
+            copies[t].wait()
+            take(pl.ds(t * 256, 256), times_t(left[...], unit[t]))
+        spent(2.5)
+
+    def into_total(q):
+        def take(columns, value):
+            if q == 0:
+                r.total[:, columns] = value
+            else:
+                r.total[:, columns] = r.total[:, columns] + value
+
+        return take
+
+    fetched = {}
+
+    def fetch(name, source, target):
+        fetched[name] = pltpu.make_async_copy(source, target, r.s_fetch.at[len(fetched)])
+        fetched[name].start()
+
+    def arrived(*wanted_names):
+        for name in wanted_names:
+            fetched[name].wait()
+
+    xs, dx, total, low, act, up, du, hidden = (
+        r.xs, r.dx, r.total, r.low, r.act, r.up, r.du, r.hidden
+    )
+    fetch("x4", r.x4, xs.at[0])
+    fetch("cot", r.cot, r.cot_here)
+    for p in range(4):
+        fetch(("u2", p), r.u2.at[:, pl.ds(p * COLUMNS, COLUMNS)], up.at[p])
+    for copy in weight_copies(0):
+        copy.start()
+    fetch("x3", r.x3, xs.at[1])
+    fetch("depth", r.depth, r.depth_here)
+    fetch("gates", r.gates, r.gates_here)
+    fetch("gated", r.gated, r.gated_here)
+    fetch("qkv", r.qkv, r.qkv_here)
+    fetch("attended", r.attended, r.attended_here)
+    fetch("lens", r.lens, r.lens_here)
+    fetch("h0", r.h0, r.h0_here)
+    for j in range(8):
+        swap_start(0, j)
+    sums[...] = jnp.zeros(sums.shape, F32)
+    arrived("x4", "cot")
+
+    def frame_block(ref, rows):
+        return ref[rows.start // 64, pl.ds(pl.multiple_of(lax.rem(rows.start, 64), BLOCK), BLOCK), :]
+
+    @blocks(length, BLOCK)
+    def _(rows):
+        grad = norm_back(xs[0, rows, :], frame_block(r.cot_here, rows).astype(F32), norm, 5, sums)
+        dx[rows, :] = grad
+        low[rows, :] = (0.5 * grad).astype(BF16)
+
+    fetch("x2", r.x2, xs.at[0])
+
+    def feed_forward_back(kind, x_slot, norm_index, write):
+        arrived(*[(kind, p) for p in range(4)])
+        for p in range(4):
+
+            @pl.loop(0, 8)
+            def _(t):
+                value = up[p, :, pl.ds(pl.multiple_of(t * 128, 128), 128)].astype(F32)
+                place_at = pl.ds(pl.multiple_of((2 * p + t // 4) * 128, 128), 128)
+                hidden[lax.rem(t, 4), :, place_at] = silu(value).astype(BF16)
+
+        for q in range(4):
+            emit(hidden.at[q], low)
+        for p in range(4):
+
+            def take(columns, value, p=p):
+                du[p, :, columns] = (value * silu_back(up[p, :, columns].astype(F32))).astype(BF16)
+
+            times_matrix(low, take)
+            spent(1.0)
+        for p in range(4):
+            times_matrix(du.at[p], into_total(p))
+        write()
+        for p in range(4):
+            emit(act, du.at[p])
+
+    def block_norm(x_slot, norm_index):
+        @blocks(length, BLOCK)
+        def _(rows):
+            act[rows, :] = normalise(xs[x_slot, rows, :], norm, norm_index).astype(BF16)
+
+        spent(3.0)
+
+    def block_norm_back(x_slot, norm_index, factor):
+        @blocks(length, BLOCK)
+        def _(rows):
+            grad = dx[rows, :] + norm_back(xs[x_slot, rows, :], total[rows, :], norm, norm_index, sums)
+            dx[rows, :] = grad
+            low[rows, :] = (factor * grad).astype(BF16)
+
+        spent(5.0)
+
+    def after_two():
+        arrived("x3")
+        block_norm(1, 4)
+
+    feed_forward_back("u2", 1, 4, after_two)
+    for p in range(4):
+        fetch(("u1", p), r.u1.at[:, pl.ds(p * COLUMNS, COLUMNS)], up.at[p])
+    block_norm_back(1, 4, 1.0)
+    fetch("x1", r.x1, xs.at[1])
+
+    depth, gates, gated, spread = r.depth_here, r.gates_here, r.gated_here, r.spread
+    arrived("depth", "gated", "gates", "lens")
+    live_count = r.lens_here[0, 0:1, 0:1]
+
+    @blocks(length, BLOCK)
+    def _(rows):
+        act[rows, :] = silu(normalise(depth[rows, :], norm, 3)).astype(BF16)
+
+    emit(act, low)
+    times_matrix(low, into_total(0))
+    spread[0:8, :] = jnp.zeros((8, width), F32)
+    spread[length + 8 : length + 16, :] = jnp.zeros((8, width), F32)
+
+    @blocks(length, BLOCK)
+    def _(rows):
+        inner = depth[rows, :]
+        dy = total[rows, :] * silu_back(normalise(inner, norm, 3))
+        grad = norm_back(inner, dy, norm, 3, sums).astype(BF16).astype(F32)
+        spread[pl.ds(pl.multiple_of(rows.start, BLOCK) + 8, BLOCK), :] = grad
+
+    spent(6.0)
+
+    @blocks(length, BLOCK)
+    def _(rows):
+        around = pl.ds(pl.multiple_of(rows.start, BLOCK), BLOCK + 16)
+        near = spread[around, :]
+        passed = gated[around, :]
+        here = near[8 : 8 + BLOCK]
+        grad = jnp.zeros((BLOCK, width), F32)
+        for t in range(taps.shape[0]):
+            grad = grad + taps[t : t + 1, :] * near[10 - t : 10 - t + BLOCK]
+            product = here * passed[6 + t : 6 + t + BLOCK]
+            sums[12 + t] += jnp.sum(product.reshape(-1, 8, width), axis=0)
+        live = lax.broadcasted_iota(jnp.int32, (BLOCK, width), 0) + rows.start
+        grad = jnp.where(live.astype(F32) < live_count, grad, 0.0)
+        opened = sigmoid(gates[1, rows, :].astype(F32))
+        du[0, rows, :] = (grad * opened).astype(BF16)
+        du[1, rows, :] = (grad * gates[0, rows, :].astype(F32) * opened * (1.0 - opened)).astype(BF16)
+
+    arrived("x2")
+    spent(8.0)
+    block_norm(0, 2)
+    for p in range(2):
+        emit(act, du.at[p])
+        times_matrix(du.at[p], into_total(p))
+    block_norm_back(0, 2, 1.0)
+
+    qkv, heads_grad, sides = r.qkv_here, r.heads_grad, r.sides
+    arrived("attended", "qkv")
+    emit(r.attended_here, low)
+
+    def take(columns, value):
+        heads_grad[:, columns] = value.astype(BF16)
+
+    times_matrix(low, take)
+    for h in range(heads):
+        columns = pl.ds(h * head_dim, head_dim)
+        sides[...] = jnp.zeros(sides.shape, F32)
+
+        @blocks(length, QUERIES)
+        def _(rows, h=h, columns=columns):
+            q, k, v = qkv[0, rows, columns], qkv[1, :, columns], qkv[2, :, columns]
+            do = heads_grad[rows, columns]
+            scores, distance = score_block(q, k, slope[h : h + 1, :], rows.start, live_count)
+            prob = softmax_block(scores)
+            dp = times_t(do, v)
+            exact = prob * (dp - jnp.sum(prob * dp, axis=-1, keepdims=True))
+            sums[17 + h, :, 0:length] -= jnp.sum((exact * distance).reshape(-1, 8, length), axis=0)
+            ds = exact.astype(BF16)
+            scale = head_dim**-0.5
+            du[0, rows, columns] = (jnp.dot(ds, k, preferred_element_type=F32) * scale).astype(BF16)
+            sides[0] += t_times(ds, q) * scale
+            sides[1] += t_times(prob.astype(BF16), do)
+
+        du[1, :, columns] = sides[0].astype(BF16)
+        du[2, :, columns] = sides[1].astype(BF16)
+        spent(6.0)
+    arrived("x1")
+    block_norm(1, 1)
+    for p in range(3):
+        emit(act, du.at[p])
+        times_matrix(du.at[p], into_total(p))
+    block_norm_back(1, 1, 0.5)
+    arrived("h0")
+
+    def after_one():
+        @blocks(length, BLOCK)
+        def _(rows):
+            value = frame_block(r.h0_here, rows).astype(F32)
+            act[rows, :] = normalise(value, norm, 0).astype(BF16)
+            grad = dx[rows, :] + norm_back(value, total[rows, :], norm, 0, sums)
+            spot = pl.ds(pl.multiple_of(lax.rem(rows.start, 64), BLOCK), BLOCK)
+            r.dframes[rows.start // 64, spot, :] = grad.astype(BF16)
+
+        for i in range(17):
+            r.wide[i : i + 1, :] = jnp.sum(sums[i], axis=0, keepdims=True)
+        for h in range(heads):
+            whole = jnp.sum(jnp.sum(sums[17 + h], axis=0, keepdims=True), axis=1, keepdims=True)
+            r.wide[17 + h : 18 + h, :] = jnp.broadcast_to(whole, (1, width))
+        r.wide[17 + heads : 32, :] = jnp.zeros((15 - heads, width), F32)
+        r.small[...] = r.wide[...].astype(BF16)
+        for j in range(8):
+            swap_start(1, j)
+            swap_start(2, j)
+
+    feed_forward_back("u1", 0, 0, after_one)
+    while ticks[0] < last + 4:
+        tick()
+    for i in range(3):
+        swap_wait(i)
+
+    @pl.when(other)
+    def _():
+        for u in range(last):
+            far_copy(u, 0).wait_recv()
+            far_copy(u, 1).wait_recv()
+
+
+def backward(made, fulls, norm, taps, slope, collective_id):
+    width = norm.shape[-1]
+    length = made.x4_out.shape[0]
+    blocked = (8, length // 8, width)
+    shapes = [(f.shape[0] // 8, f.shape[1]) for f in fulls]
+    count = len(fulls)
+    units = [
+        (index, row, column)
+        for index in BACK_ORDER
+        for row in range(0, shapes[index][0], ROWS)
+        for column in range(0, shapes[index][1], COLUMNS)
+    ]
+    number = len(units)
+    dma = pltpu.SemaphoreType.DMA
+    given = dict(
+        cot=made.cot_out,
+        h0=made.h0_out,
+        u1=made.u1_out,
+        x1=made.x1_out,
+        qkv=made.qkv_out,
+        attended=made.attended_out,
+        x2=made.x2_out,
+        gates=made.gates_out,
+        gated=made.gated_out,
+        depth=made.depth_out,
+        x3=made.x3_out,
+        u2=made.u2_out,
+        x4=made.x4_out,
+        result=made.result_out.reshape(blocked),
+        lens=made.lens_out,
+    )
+    outs = dict(
+        result_home=jax.ShapeDtypeStruct(blocked, BF16),
+        dframes_home=jax.ShapeDtypeStruct(blocked, BF16),
+        small_home=jax.ShapeDtypeStruct((8, 32, width), BF16),
+    )
+    scratch = dict(
+        xs=pltpu.VMEM((2, length, width), F32),
+        dx=pltpu.VMEM((length, width), F32),
+        total=pltpu.VMEM((length, width), F32),
+        low=pltpu.VMEM((length, width), BF16),
+        act=pltpu.VMEM((length, width), BF16),
+        up=pltpu.VMEM((4, length, width), BF16),
+        du=pltpu.VMEM((4, length, width), BF16),
+        hidden=pltpu.VMEM((4, length, width), BF16),
+        cot_here=pltpu.VMEM(blocked, BF16),
+        h0_here=pltpu.VMEM(blocked, BF16),
+        dframes=pltpu.VMEM(blocked, BF16),
+        depth_here=pltpu.VMEM((length, width), F32),
+        gates_here=pltpu.VMEM((2, length, width), BF16),
+        gated_here=pltpu.VMEM((length + 16, width), F32),
+        spread=pltpu.VMEM((length + 16, width), F32),
+        qkv_here=pltpu.VMEM((3, length, width), BF16),
+        attended_here=pltpu.VMEM((length, width), BF16),
+        heads_grad=pltpu.VMEM((length, width), BF16),
+        sides=pltpu.VMEM((2, length, width // slope.shape[0]), F32),
+        lens_here=pltpu.VMEM(made.lens_out.shape, F32),
+        sums=pltpu.VMEM((17 + slope.shape[0], 8, width), F32),
+        wide=pltpu.VMEM((32, width), F32),
+        small=pltpu.VMEM((32, width), BF16),
+        unit=pltpu.VMEM((2, 4, 256, 1024), BF16),
+        stage=pltpu.VMEM((2, 4, 2, ROWS, COLUMNS), BF16),
+        mine=pltpu.VMEM((SLOTS, 4, 2, HALF, COLUMNS), BF16),
+        core_in=pltpu.VMEM((2, 4, 2, HALF, COLUMNS), BF16),
+        first_in=pltpu.VMEM((SLOTS, 4, HALF, COLUMNS), BF16),
+        second_in=pltpu.VMEM((SLOTS, 2, HALF, COLUMNS), BF16),
+        s_unit=dma((2, 4)),
+        s_stage=dma((2,)),
+        s_fetch=dma((32,)),
+        swap_send=dma((3, 8)),
+        swap_recv=dma((3, 8)),
+        swap_own=dma((3,)),
+        s_load=dma((2,)),
+        s_core=dma((2,)),
+        r_core=dma((2,)),
+        s_first=dma((SLOTS, 2)),
+        r_first=dma((SLOTS, 2)),
+        s_second=dma((SLOTS, 2)),
+        r_second=dma((SLOTS, 2)),
+        s_far=dma((2,)),
+        r_far=dma((number, 2)),
+        s_near=dma((2,)),
+        r_near=dma((number,)),
+        s_own=dma((2,)),
+    )
+    vmem = pl.BlockSpec(memory_space=pltpu.VMEM)
+    operands = dict(given, norm=norm, taps=taps, slope=slope)
+
+    def body(*refs):
+        refs = list(refs)
+        cut = lambda n: [refs.pop(0) for _ in range(n)]
+        plain, full_refs, made_refs = cut(len(operands)), cut(count), cut(len(outs))
+        out_refs, grad_refs = cut(count), cut(count)
+        backward_kernel(
+            units,
+            list(operands) + list(outs) + list(scratch) + ["fulls", "outs", "grads"],
+            *plain,
+            *made_refs,
+            *refs,
+            full_refs,
+            out_refs,
+            grad_refs,
+        )
+
+    results = pl.pallas_call(
+        body,
+        out_shape=list(outs.values())
+        + [jax.ShapeDtypeStruct(s, BF16) for s in shapes]
+        + [jax.ShapeDtypeStruct((4, 2) + s, BF16) for s in shapes],
+        in_specs=[ANY] * len(given) + [vmem] * 3 + [ANY] * count,
+        out_specs=[ANY] * (len(outs) + 2 * count),
+        scratch_shapes=list(scratch.values()),
+        compiler_params=pltpu.CompilerParams(
+            collective_id=collective_id, has_side_effects=True, vmem_limit_bytes=62 * 2**20
+        ),
+    )(*operands.values(), *fulls)
+    return results[: len(outs)], results[len(outs) : len(outs) + count]
+
+
+def per_device(
+    frames_in,
+    noise,
+    lengths,
+    span_starts,
+    w_in1,
+    w_out1,
+    w_qkv,
+    w_attn,
+    w_point1,
+    w_point2,
+    w_in2,
+    w_out2,
+    norm_params,
+    kernel,
+    slopes,
+    cotangent,
+):
+    utterances, frames, width = frames_in.shape
+    heads = slopes.shape[0]
+    length = frames * 8
+    frame_pos = lax.axis_index("seq") * frames + jnp.arange(frames, dtype=jnp.int32)
+    span_begin = span_starts[:, :, None]
+    masked = jnp.any(
+        (span_begin <= frame_pos[None, None, :]) & (frame_pos[None, None, :] < span_begin + SPAN),
+        axis=1,
+    )
+    start = jnp.where(masked[..., None], noise, frames_in)
+    lens = jnp.broadcast_to(lengths.astype(F32)[:, None, None], (utterances, 8, 128))
+    slope_rows = jnp.broadcast_to(slopes[:, None], (heads, length))
+    shards = (w_in1, w_out1, w_qkv, w_attn, w_point1, w_point2, w_in2, w_out2)
+    made, fulls = forward(start, lens, cotangent, norm_params, kernel, slope_rows, shards, 0)
+    (block_out, dframes, small), grads = backward(made, fulls, norm_params, kernel, slope_rows, 1)
+    small = jnp.sum(small.astype(F32), axis=0)
+    grad_frames = jnp.where(masked[..., None], 0.0, dframes.astype(F32))
+    return (
+        block_out,
+        grad_frames,
+        *[grad.astype(F32) for grad in grads],
+        small[:12].reshape(6, 2, width),
+        small[12:17],
+        small[17 : 17 + heads, 0],
+    )
+
+
 def solution(mesh):
     in_specs = (
         P("dp", "seq", None),
@@ -410,6 +1659,7 @@
         P("dp", None),
         P("dp"),
     )
+    grouped = mesh.shape["seq"] == 8 and mesh.shape["dp"] == 4
     return jax.shard_map(
-        per_device, mesh=mesh, in_specs=in_specs, out_specs=out_specs, check_vma=False
-    )
+        per_device if grouped else per_device_any, mesh=mesh, in_specs=in_specs, out_specs=out_specs, check_vma=False
+    )

time: 2190 us -> 621 us (0.28)
  waiting for transfers between devices: 1720 us -> 0 us
  Pallas kernels: 0 us -> 585 us
  matrix products: 234 us -> 0 us
  blocking collectives: 97.6 us -> 0 us
  local copies, waits for them, and re-layouts: 58.9 us -> 4.92 us
  other arithmetic: 48 us -> 19.7 us
    all_gather x12 -> x0, waiting for transfers between devices: 1030 us -> none  [the longest x1 125 us: per_device(): lax.all_gather(shards[0], 'seq', axis=0, tiled=True)]
    reduce_scatter x2 -> x0, waiting for transfers between devices: 678 us -> none  [per_device(): lax.psum_scatter(jnp.concatenate([matmul_left_t(left_side, right_side) fo...]
    pallas_call x0 -> x2, Pallas kernels: none -> 585 us  [the longest x1 324 us: backward(): pl.pallas_call(body, out_shape=list(outs.values()) + [jax.ShapeDtypeStruc...]
    dot_general x31 -> x0, matrix products: 234 us -> none  [the longest x8 61.5 us: matmul(): return jnp.dot(left_side, right_side, preferred_element_type=jnp.float32)]
    all_gather x2 -> x0, blocking collectives: 67 us -> none  [the longest x1 34.9 us: per_device(): lax.all_gather(log_total.astype(jnp.bfloat16), 'seq', axis=1, tiled=True)]
    unnamed x219 -> x17, local copies, waits for them, and re-layouts: 33.9 us -> 1 us
    psum x1 -> x0, blocking collectives: 30.6 us -> none  [per_device(): lax.psum(grad_norms.astype(jnp.bfloat16), 'seq').astype(jnp.float32)]
  transfers between devices with their start and end apart: 18 -> 0, of which waited for: 16 -> 0; matrix products, arithmetic and copies ran while one was open for 11% -> 0% of each run, Pallas kernels for 0% -> 0%
where the time goes in v3:
time: 621 us; the launch traced here: 611 us
  Pallas kernels  585 us (94%)
  other arithmetic  19.7 us (3%)
    pallas_call x1, Pallas kernels, backward(): pl.pallas_call(body, out_shape=list(outs.values()) + [jax.ShapeDtypeStruc...  324 us
    pallas_call x1, Pallas kernels, forward(): pl.pallas_call(body, out_shape=list(outs.values()) + [jax.ShapeDtypeStruc...  261 us

profile of v3, /device:TPU:1, one launch (start us, length us, event | category | flops | bytes accessed | tf_op | source)
XLA Modules:
  0.0 610.8 jit_solution(15909340904803584174)
XLA Ops:
  0.7 0.7 convert_element_type.33
  1.3 0.7 broadcast_add_fusion
  2.0 0.8 and_reduce_fusion
  2.8 1.3 broadcast_in_dim.20.refs_5_.refs_17_
  4.1 0.7 broadcast_in_dim.19.refs_1_
  4.8 2.7 broadcast_select_fusion.refs_0_
  7.5 261.2 %shard_map.255 = (bf16[8,64,1024]{2,1,0:T(8,128)(2,1)}, bf16[8,64,1024]{2,1,0:T(8,128)(2,1)}, bf16[512,4096]{1,0:T(8,128)(2,1)}, f32[512,1024]{1,0:T(8,128)}, bf...) custom-call(bf16[8,64,1024]{2,1,0:T(8,128)(2,1)} %broadcast_select_f, ...), custom_call_target="tpu_custom_call" | custom-call | tf_op jit(solution)/shard_map/pallas_call | solution.py:921
  268.7 323.9 %shard_map.256 = (bf16[8,64,1024]{2,1,0:T(8,128)(2,1)}, bf16[8,64,1024]{2,1,0:T(8,128)(2,1)}, bf16[8,32,1024]{2,1,0:T(8,128)(2,1)}, bf16[128,4096]{1,0:T(8,128)(...) custom-call(bf16[8,64,1024]{2,1,0:T(8,128)(2,1)} %get-tuple-element., ...), custom_call_target="tpu_custom_call" | custom-call | tf_op jit(solution)/shard_map/pallas_call | solution.py:1568
  592.6 1.2 convert_reduce_fusion
  593.8 0.6 slice_reduce_fusion
  594.5 0.6 slice.13
  595.1 0.7 reshape.75
  595.7 1.8 convert_element_type.38
  597.5 1.8 convert_element_type.40
  599.3 0.0 copy-done.7
  599.3 1.1 convert_element_type.39
  600.4 1.3 convert_element_type.37
  601.7 1.5 convert_select_fusion
  603.2 1.5 convert_element_type.35
  604.8 1.6 convert_element_type.36
  606.3 1.5 convert_element_type.41
  607.9 1.6 convert_element_type.42
  609.4 0.0 copy-done.4
  609.4 1.0 copy.30
  (16 shorter events, 0.0 us)
Async XLA Ops:
  592.6 6.7 %copy-start.7 = (bf16[128,2048]{1,0:T(8,128)(2,1)S(1)}, bf16[128,2048]{1,0:T(8,128)(2,1)}, u32[]{:S(2)}) copy-start(bf16[128,2048]{1,0:T(8,128)(2,1)} %get-tuple-element.76) | copy-start | bytes 1572868
  592.6 7.8 %copy-start.6 = (bf16[128,3072]{1,0:T(8,128)(2,1)S(1)}, bf16[128,3072]{1,0:T(8,128)(2,1)}, u32[]{:S(2)}) copy-start(bf16[128,3072]{1,0:T(8,128)(2,1)} %get-tuple-element.74) | copy-start | bytes 2359300
  599.3 2.4 copy-start.5
  601.7 1.5 copy-start.3
  603.2 1.5 copy-start.2
  604.8 1.6 copy-start.1
  606.3 1.5 copy-start
  607.9 1.6 copy-start.4

commit v4 on v3

--- a/solution.py
+++ b/solution.py
@@ -665,7 +665,7 @@
         return act_on
 
     for step in range(last + LAGS[-1]):
-        for depth, lag in enumerate(LAGS):
+        for depth, lag in reversed(list(enumerate(LAGS))):
             if 0 <= step - lag < last:
                 actions.append(move(step - lag, depth))
                 if depth == len(stages):
@@ -934,7 +934,7 @@
 
 
 CADENCE = 12.0
-SLOTS = 5
+SLOTS = 7
 
 
 def norm_back(v, dy, norm, i, sums):
@@ -998,7 +998,7 @@
 
     pl.semaphore_wait(barrier, jnp.where(keeps, 11, 12))
 
-    swaps = ((r.result, r.result_home), (r.dframes, r.dframes_home), (r.small, r.small_home))
+    swaps = ((r.result, r.result_home), (r.cot_here, r.dframes_home), (r.small, r.small_home))
 
     def swap(i, j):
         source, target = swaps[i][0], swaps[i][1].at[utterance]
@@ -1161,7 +1161,7 @@
         def _():
             near_copy(u, half).wait_send()
 
-    order = ((stage1, 1), (stage0, 0), (stage2, 2), (stage3, 3), (stage4, 4))
+    order = ((stage1, 1), (stage0, 0), (stage2, 3), (stage3, 5), (stage4, 6))
     ticks, emitted, clock = [0], [0], [0.0]
 
     def tick():
@@ -1390,7 +1390,7 @@
         times_matrix(du.at[p], into_total(p))
     block_norm_back(0, 2, 1.0)
 
-    qkv, heads_grad, sides = r.qkv_here, r.heads_grad, r.sides
+    qkv, heads_grad, sides = r.qkv_here, act, r.sides
     arrived("attended", "qkv")
     emit(r.attended_here, low)
 
@@ -1435,7 +1435,7 @@
             act[rows, :] = normalise(value, norm, 0).astype(BF16)
             grad = dx[rows, :] + norm_back(value, total[rows, :], norm, 0, sums)
             spot = pl.ds(pl.multiple_of(lax.rem(rows.start, 64), BLOCK), BLOCK)
-            r.dframes[rows.start // 64, spot, :] = grad.astype(BF16)
+            r.cot_here[rows.start // 64, spot, :] = grad.astype(BF16)
 
         for i in range(17):
             r.wide[i : i + 1, :] = jnp.sum(sums[i], axis=0, keepdims=True)
@@ -1449,7 +1449,7 @@
             swap_start(2, j)
 
     feed_forward_back("u1", 0, 0, after_one)
-    while ticks[0] < last + 4:
+    while ticks[0] < last + 6:
         tick()
     for i in range(3):
         swap_wait(i)
@@ -1508,14 +1508,12 @@
         hidden=pltpu.VMEM((4, length, width), BF16),
         cot_here=pltpu.VMEM(blocked, BF16),
         h0_here=pltpu.VMEM(blocked, BF16),
-        dframes=pltpu.VMEM(blocked, BF16),
         depth_here=pltpu.VMEM((length, width), F32),
         gates_here=pltpu.VMEM((2, length, width), BF16),
         gated_here=pltpu.VMEM((length + 16, width), F32),
         spread=pltpu.VMEM((length + 16, width), F32),
         qkv_here=pltpu.VMEM((3, length, width), BF16),
         attended_here=pltpu.VMEM((length, width), BF16),
-        heads_grad=pltpu.VMEM((length, width), BF16),
         sides=pltpu.VMEM((2, length, width // slope.shape[0]), F32),
         lens_here=pltpu.VMEM(made.lens_out.shape, F32),
         sums=pltpu.VMEM((17 + slope.shape[0], 8, width), F32),

time: 621 us -> 601 us (0.968)
  Pallas kernels: 585 us -> 565 us
    pallas_call x1, Pallas kernels: 324 us -> 305 us  [backward(): pl.pallas_call(body, out_shape=list(outs.values()) + [jax.ShapeDtypeStruc...]
where the time goes in v4:
time: 601 us; the launch traced here: 591 us
  Pallas kernels  565 us (94%)
  other arithmetic  19.7 us (3%)
    pallas_call x1, Pallas kernels, backward(): pl.pallas_call(body, out_shape=list(outs.values()) + [jax.ShapeDtypeStruc...  305 us
    pallas_call x1, Pallas kernels, forward(): pl.pallas_call(body, out_shape=list(outs.values()) + [jax.ShapeDtypeStruc...  260 us
    convert_element_type x8, other arithmetic, per_device(): grad.astype(F32)  12.1 us

profile of v4, /device:TPU:1, one launch (start us, length us, event | category | flops | bytes accessed | tf_op | source)
XLA Modules:
  0.0 591.0 jit_solution(1815820051090536539)
XLA Ops:
  0.7 0.7 convert_element_type.33
  1.3 0.7 broadcast_add_fusion
  2.0 0.8 and_reduce_fusion
  2.8 1.3 broadcast_in_dim.20.refs_5_.refs_17_
  4.1 0.7 broadcast_in_dim.19.refs_1_
  4.8 2.7 broadcast_select_fusion.refs_0_
  7.5 259.9 %shard_map.255 = (bf16[8,64,1024]{2,1,0:T(8,128)(2,1)}, bf16[8,64,1024]{2,1,0:T(8,128)(2,1)}, bf16[512,4096]{1,0:T(8,128)(2,1)}, f32[512,1024]{1,0:T(8,128)}, bf...) custom-call(bf16[8,64,1024]{2,1,0:T(8,128)(2,1)} %broadcast_select_f, ...), custom_call_target="tpu_custom_call" | custom-call | tf_op jit(solution)/shard_map/pallas_call | solution.py:921
  267.4 305.3 %shard_map.256 = (bf16[8,64,1024]{2,1,0:T(8,128)(2,1)}, bf16[8,64,1024]{2,1,0:T(8,128)(2,1)}, bf16[8,32,1024]{2,1,0:T(8,128)(2,1)}, bf16[128,4096]{1,0:T(8,128)(...) custom-call(bf16[8,64,1024]{2,1,0:T(8,128)(2,1)} %get-tuple-element., ...), custom_call_target="tpu_custom_call" | custom-call | tf_op jit(solution)/shard_map/pallas_call | solution.py:1566
  572.8 0.0 copy-start.7
  572.8 1.2 convert_reduce_fusion
  574.0 0.6 slice_reduce_fusion
  574.6 0.6 slice.13
  575.3 0.7 reshape.75
  575.9 1.8 convert_element_type.38
  577.7 1.8 convert_element_type.40
  579.5 1.1 convert_element_type.39
  580.6 1.3 convert_element_type.37
  581.9 1.5 convert_select_fusion
  583.4 1.5 convert_element_type.35
  585.0 1.6 convert_element_type.36
  586.5 0.0 copy-done.1
  586.5 1.5 convert_element_type.41
  588.1 1.6 convert_element_type.42
  589.6 1.0 copy.30
  (16 shorter events, 0.0 us)
Async XLA Ops:
  572.8 6.7 %copy-start.7 = (bf16[128,2048]{1,0:T(8,128)(2,1)S(1)}, bf16[128,2048]{1,0:T(8,128)(2,1)}, u32[]{:S(2)}) copy-start(bf16[128,2048]{1,0:T(8,128)(2,1)} %get-tuple-element.76) | copy-start | bytes 1572868
  572.8 7.8 %copy-start.6 = (bf16[128,3072]{1,0:T(8,128)(2,1)S(1)}, bf16[128,3072]{1,0:T(8,128)(2,1)}, u32[]{:S(2)}) copy-start(bf16[128,3072]{1,0:T(8,128)(2,1)} %get-tuple-element.74) | copy-start | bytes 2359300
  579.5 2.4 copy-start.5
  581.9 1.5 copy-start.3
  583.4 1.5 copy-start.2
  585.0 1.6 copy-start.1
  586.5 1.5 copy-start
  588.1 1.6 copy-start.4

commit v5 on v4

--- a/solution.py
+++ b/solution.py
@@ -719,8 +719,12 @@
 
     keep(r.h0, r.h0_out)
 
-    def feed_forward(x_in, x_out, up, up_out):
+    hidden_kept = []
+
+    def feed_forward(x_in, x_out, up, up_out, hidden_out):
         hidden = r.hidden
+        for copy in hidden_kept:
+            copy.wait()
         for p in range(4):
             unit, loads = weight()
 
@@ -736,6 +740,8 @@
                 poll()
 
             keep(up.at[p], up_out.at[:, pl.ds(p * COLUMNS, COLUMNS)])
+        hidden_kept[:] = [pltpu.make_async_copy(hidden, hidden_out, r.kept.at[31])]
+        hidden_kept[0].start()
         for q in range(4):
             def emit(columns, value, q=q):
                 if q == 0:
@@ -749,7 +755,7 @@
         def _(rows):
             xs[x_out, rows, :] = xs[x_in, rows, :] + 0.5 * acc[rows, :]
 
-    feed_forward(0, 1, r.up, r.u1_out)
+    feed_forward(0, 1, r.up, r.u1_out, r.s1_out)
     keep(xs.at[1], r.x1_out)
 
     @blocks(length, BLOCK)
@@ -834,7 +840,7 @@
     def _(rows):
         act[rows, :] = normalise(xs[3, rows, :], norm, 4).astype(BF16)
 
-    feed_forward(3, 4, r.up2, r.u2_out)
+    feed_forward(3, 4, r.up2, r.u2_out, r.s2_out)
     keep(xs.at[4], r.x4_out)
 
     @blocks(length, BLOCK)
@@ -843,7 +849,7 @@
 
     keep(act, r.result_out)
     swap_wait(2)
-    for copy in kept:
+    for copy in hidden_kept + kept:
         copy.wait()
 
 
@@ -874,6 +880,8 @@
         u2_out=up,
         x4_out=wide(),
         result_out=low(),
+        s1_out=low(4),
+        s2_out=low(4),
         lens_out=jax.ShapeDtypeStruct(lens.shape, lens.dtype),
     )
     scratch = dict(
@@ -1264,6 +1272,7 @@
     )
     fetch("x4", r.x4, xs.at[0])
     fetch("cot", r.cot, r.cot_here)
+    fetch("s2", r.s2, hidden)
     for p in range(4):
         fetch(("u2", p), r.u2.at[:, pl.ds(p * COLUMNS, COLUMNS)], up.at[p])
     for copy in weight_copies(0):
@@ -1292,18 +1301,11 @@
 
     fetch("x2", r.x2, xs.at[0])
 
-    def feed_forward_back(kind, x_slot, norm_index, write):
-        arrived(*[(kind, p) for p in range(4)])
-        for p in range(4):
-
-            @pl.loop(0, 8)
-            def _(t):
-                value = up[p, :, pl.ds(pl.multiple_of(t * 128, 128), 128)].astype(F32)
-                place_at = pl.ds(pl.multiple_of((2 * p + t // 4) * 128, 128), 128)
-                hidden[lax.rem(t, 4), :, place_at] = silu(value).astype(BF16)
-
+    def feed_forward_back(kind, stored_as, write):
+        arrived(stored_as)
         for q in range(4):
             emit(hidden.at[q], low)
+        arrived(*[(kind, p) for p in range(4)])
         for p in range(4):
 
             def take(columns, value, p=p):
@@ -1337,7 +1339,8 @@
         arrived("x3")
         block_norm(1, 4)
 
-    feed_forward_back("u2", 1, 4, after_two)
+    feed_forward_back("u2", "s2", after_two)
+    fetch("s1", r.s1, hidden)
     for p in range(4):
         fetch(("u1", p), r.u1.at[:, pl.ds(p * COLUMNS, COLUMNS)], up.at[p])
     block_norm_back(1, 4, 1.0)
@@ -1448,7 +1451,7 @@
             swap_start(1, j)
             swap_start(2, j)
 
-    feed_forward_back("u1", 0, 0, after_one)
+    feed_forward_back("u1", "s1", after_one)
     while ticks[0] < last + 6:
         tick()
     for i in range(3):
@@ -1488,6 +1491,8 @@
         depth=made.depth_out,
         x3=made.x3_out,
         u2=made.u2_out,
+        s1=made.s1_out,
+        s2=made.s2_out,
         x4=made.x4_out,
         result=made.result_out.reshape(blocked),
         lens=made.lens_out,

time: 601 us -> 601 us (level)
  no operation moved by 1% of the time
where the time goes in v5:
time: 601 us; the launch traced here: 591 us
  Pallas kernels  565 us (94%)
  other arithmetic  19.7 us (3%)
    pallas_call x1, Pallas kernels, backward(): pl.pallas_call(body, out_shape=list(outs.values()) + [jax.ShapeDtypeStruc...  305 us
    pallas_call x1, Pallas kernels, forward(): pl.pallas_call(body, out_shape=list(outs.values()) + [jax.ShapeDtypeStruc...  260 us
    convert_element_type x8, other arithmetic, per_device(): grad.astype(F32)  12.1 us

profile of v5, /device:TPU:1, one launch (start us, length us, event | category | flops | bytes accessed | tf_op | source)
XLA Modules:
  0.0 590.7 jit_solution(7800359949169798727)
XLA Ops:
  0.7 0.7 convert_element_type.33
  1.3 0.7 broadcast_add_fusion
  2.0 0.8 and_reduce_fusion
  2.8 1.3 broadcast_in_dim.20.refs_5_.refs_19_
  4.1 0.7 broadcast_in_dim.19.refs_1_
  4.8 2.7 broadcast_select_fusion.refs_0_
  7.5 259.7 %shard_map.255 = (bf16[8,64,1024]{2,1,0:T(8,128)(2,1)}, bf16[8,64,1024]{2,1,0:T(8,128)(2,1)}, bf16[512,4096]{1,0:T(8,128)(2,1)}, f32[512,1024]{1,0:T(8,128)}, bf...) custom-call(bf16[8,64,1024]{2,1,0:T(8,128)(2,1)} %broadcast_select_f, ...), custom_call_target="tpu_custom_call" | custom-call | tf_op jit(solution)/shard_map/pallas_call | solution.py:929
  267.3 305.2 %shard_map.256 = (bf16[8,64,1024]{2,1,0:T(8,128)(2,1)}, bf16[8,64,1024]{2,1,0:T(8,128)(2,1)}, bf16[8,32,1024]{2,1,0:T(8,128)(2,1)}, bf16[128,4096]{1,0:T(8,128)(...) custom-call(bf16[8,64,1024]{2,1,0:T(8,128)(2,1)} %get-tuple-element., ...), custom_call_target="tpu_custom_call" | custom-call | tf_op jit(solution)/shard_map/pallas_call | solution.py:1571
  572.5 0.0 copy-start.7
  572.5 1.2 convert_reduce_fusion
  573.7 0.6 slice_reduce_fusion
  574.3 0.6 slice.13
  575.0 0.7 reshape.75
  575.6 1.8 convert_element_type.38
  577.4 1.8 convert_element_type.40
  579.2 1.1 convert_element_type.39
  580.3 1.3 convert_element_type.37
  581.6 1.5 convert_select_fusion
  583.1 1.5 convert_element_type.35
  584.7 1.6 convert_element_type.36
  586.2 0.0 copy-done.1
  586.2 1.5 convert_element_type.41
  587.8 1.6 convert_element_type.42
  589.3 1.0 copy.30
  (16 shorter events, 0.0 us)
Async XLA Ops:
  572.5 6.7 %copy-start.7 = (bf16[128,2048]{1,0:T(8,128)(2,1)S(1)}, bf16[128,2048]{1,0:T(8,128)(2,1)}, u32[]{:S(2)}) copy-start(bf16[128,2048]{1,0:T(8,128)(2,1)} %get-tuple-element.80) | copy-start | bytes 1572868
  572.5 7.8 %copy-start.6 = (bf16[128,3072]{1,0:T(8,128)(2,1)S(1)}, bf16[128,3072]{1,0:T(8,128)(2,1)}, u32[]{:S(2)}) copy-start(bf16[128,3072]{1,0:T(8,128)(2,1)} %get-tuple-element.78) | copy-start | bytes 2359300
  579.2 2.4 copy-start.5
  581.6 1.5 copy-start.3
  583.1 1.5 copy-start.2
  584.7 1.6 copy-start.1
  586.2 1.5 copy-start
  587.8 1.6 copy-start.4
